TPU v7x, 512 devices: a whole 4x4x16 slice. The times are simulated.
512 devices in a mesh: dp: 64 (over z, x), cuts: 8 (over y, core).
Axes of the slice: x: 4, y: 4, z: 16, core: 2. Of those that a mesh axis runs over, the one named last changes fastest.
Arguments:
- queries: bfloat16 [512, 2048], P('dp', 'cuts'), may hold values from -240 to 240
- new_keys: bfloat16 [512, 2048], P('dp', 'cuts'), may hold values from -6 to 6
- new_values: bfloat16 [512, 2048], P('dp', 'cuts'), may hold values from -6 to 6
- key_cache: bfloat16 [512, 64, 2048], P('dp', None, 'cuts'), may hold values from -6 to 6
- value_cache: bfloat16 [512, 64, 2048], P('dp', None, 'cuts'), may hold values from -6 to 6
- lengths: int32 [512], P('dp'), may hold values from 1 to 64
- resid: bfloat16 [512, 2048], P('dp'), may hold values from -6 to 6
- norm_gain: float32 [2048], replicated, may hold values from 0.5 to 1.5
- w_out: bfloat16 [2048, 2048], P('cuts'), may hold values from -0.125 to 0.125
- experts: int32 [512, 1], P('dp'), may hold values from 0 to 15; in each aligned block of 8 rows (0 to 7, 8 to 15, ...) at most 2 rows name the same one
- w_up: bfloat16 [64, 2048, 2048], P('dp', None, 'cuts'), may hold values from -0.125 to 0.125
- w_down: bfloat16 [64, 2048, 2048], P('dp', 'cuts'), may hold values from -0.0625 to 0.0625
Outputs:
- mixed: bfloat16 [512, 2048], P('dp', 'cuts')
Inputs may be any that keep to these rules, and one draw needn't show every extreme that they name: `experts`: among the 8 rows of one dp index each expert is named by at most 2 rows, and by exactly 2 in some.
All inputs are finite; a program needn't handle non-finite values.
Results may differ from a plain program's by a relative error of at most 0.014.
Values may be sent and summed in bfloat16 or wider, within the bound.
No kernel may reach another device: no remote copies, remote signals or barrier semaphores. Data moves between devices by JAX's collectives and lax.ppermute only.
A program may use at most 64 MiB of HBM per device.

v0:
```python
import jax
import jax.numpy as jnp
from jax import lax
from jax.sharding import PartitionSpec as P

HD = 128
GROUP = 4


def attend_local(queries, new_keys, new_values, key_cache, value_cache, lengths):
    count, feats = queries.shape
    heads = feats // HD
    length = key_cache.shape[1]
    scale = 1.0 / HD**0.5
    query = queries.reshape(count, heads, HD)
    kcache = key_cache.reshape(count, length, heads, HD)
    vcache = value_cache.reshape(count, length, heads, HD)
    nkey = new_keys.reshape(count, heads, HD)
    nval = new_values.reshape(count, heads, HD)
    scores = jnp.einsum("rhd,rjhd->rhj", query, kcache, preferred_element_type=jnp.float32) * scale
    keep = jnp.arange(length)[None, None, :] < lengths[:, None, None]
    scores = jnp.where(keep, scores, -1e30)
    fresh = jnp.einsum("rhd,rhd->rh", query, nkey, preferred_element_type=jnp.float32) * scale
    peak = jnp.maximum(jnp.max(scores, axis=-1), fresh)
    pcache = jnp.where(keep, jnp.exp(scores - peak[..., None]), 0.0)
    pnew = jnp.exp(fresh - peak)
    total = jnp.sum(pcache, axis=-1) + pnew
    pcache = (pcache / total[..., None]).astype(jnp.bfloat16)
    pnew = (pnew / total).astype(jnp.bfloat16)
    summed = jnp.einsum("rhj,rjhd->rhd", pcache, vcache, preferred_element_type=jnp.float32)
    summed = summed + pnew.astype(jnp.float32)[..., None] * nval.astype(jnp.float32)
    return summed.reshape(count, feats).astype(jnp.bfloat16)


def on_device(
    queries,
    new_keys,
    new_values,
    key_cache,
    value_cache,
    lengths,
    resid,
    norm_gain,
    w_out,
    experts,
    w_up,
    w_down,
):
    count = resid.shape[0]
    width_all = resid.shape[1]
    n_cuts = lax.axis_size("cuts")
    n_data = lax.axis_size("dp")
    width = width_all // n_cuts
    cut = lax.axis_index("cuts")
    heads_out = attend_local(queries, new_keys, new_values, key_cache, value_cache, lengths)
    partial_attn = jnp.dot(heads_out, w_out, preferred_element_type=jnp.float32)
    gain_cols = lax.dynamic_slice_in_dim(norm_gain, cut * width, width, 0)
    attn = lax.psum(partial_attn, "cuts")
    hidden = resid.astype(jnp.float32) + attn
    meansq = jnp.mean(hidden * hidden, axis=-1)
    hidden_cols = lax.dynamic_slice_in_dim(hidden, cut * width, width, 1)
    normed_cols = (hidden_cols * lax.rsqrt(meansq + 1e-06)[:, None] * gain_cols[None, :]).astype(
        jnp.bfloat16
    )
    n_experts = n_data // GROUP
    slots = max(2, 2 * count * GROUP // n_data)
    ids = experts[:, 0]
    order_idx = jnp.arange(count, dtype=jnp.int32)
    earlier = (ids[:, None] == ids[None, :]) & (order_idx[:, None] > order_idx[None, :])
    slot = jnp.sum(earlier.astype(jnp.int32), axis=1)
    slot_id = ids * slots + slot
    table = jnp.arange(n_experts * slots, dtype=jnp.int32)[:, None] == slot_id[None, :]
    full_rows = lax.all_gather(normed_cols, "cuts", axis=1, tiled=True)
    packed = jnp.dot(
        table.astype(jnp.bfloat16), full_rows, preferred_element_type=jnp.float32
    ).astype(jnp.bfloat16)
    packed = packed.reshape(n_experts, slots, full_rows.shape[1])
    received = lax.all_to_all(
        jnp.repeat(packed, GROUP, axis=0), "dp", split_axis=0, concat_axis=0, tiled=True
    )
    arrived = received.reshape(n_data * slots, width_all)
    act = jax.nn.gelu(jnp.dot(arrived, w_up[0], preferred_element_type=jnp.float32)).astype(
        jnp.bfloat16
    )
    lower = w_down[0]
    share = lax.psum_scatter(
        lax.dot_general(
            lower, act, (((0,), (1,)), ((), ())), preferred_element_type=jnp.float32
        ).astype(jnp.bfloat16),
        "cuts",
        scatter_dimension=0,
        tiled=True,
    )
    outgoing = share.reshape(width, n_data, slots)
    returned = lax.all_to_all(outgoing, "dp", split_axis=1, concat_axis=1, tiled=True)
    grouped = returned.astype(jnp.float32).reshape(width, n_experts, GROUP, slots)
    combined = jnp.sum(grouped, axis=2).reshape(width, n_experts * slots)
    expert_cols = jnp.einsum(
        "ck,kr->rc", combined, table.astype(jnp.float32), precision=lax.Precision.HIGHEST
    )
    return (hidden_cols + expert_cols).astype(jnp.bfloat16)


def solution(mesh):
    placed = (
        P("dp", "cuts"),
        P("dp", "cuts"),
        P("dp", "cuts"),
        P("dp", None, "cuts"),
        P("dp", None, "cuts"),
        P("dp"),
        P("dp", None),
        P(),
        P("cuts", None),
        P("dp", None),
        P("dp", None, "cuts"),
        P("dp", "cuts", None),
    )
    return jax.shard_map(
        on_device, mesh=mesh, in_specs=placed, out_specs=P("dp", "cuts"), check_vma=False
    )
```

profile of v0, /device:TPU:1, one launch (start us, length us, event | category | flops | bytes accessed | tf_op | source)
XLA Modules:
  0.0 221.3 jit_solution(7773891441416346736)
XLA Ops:
  6.5 0.0 copy-start
  6.5 0.0 all-reduce.2.cloned.1.call-start
  6.5 0.8 iota_compare_fusion.4
  7.4 0.0 copy-start.4
  7.4 0.0 copy-start.5
  7.4 0.8 fusion.31
  8.2 0.0 copy-done.4
  8.2 1.2 fusion.8
  9.4 0.1 fusion.38
  9.5 0.2 fusion.37
  9.7 0.1 fusion.45
  9.8 0.0 copy-done.5
  9.8 0.0 copy-start.3
  9.8 0.2 fusion.5
  10.0 0.5 copy-done.3
  10.5 2.1 fusion.40
  12.6 0.0 copy-start.2
  12.6 0.0 all-reduce.2.cloned.1.call-update
  12.6 0.0 copy-start.6
  12.6 0.0 reduce-scatter.2.cloned.1.call-start
  12.7 0.6 copy-done.6
  13.3 0.2 convert_reduce_fusion.1
  13.5 0.8 dynamic_slice.7
  14.2 76.7 %all-reduce.2.cloned.1.call-done = f32[8,2048]{1,0:T(8,128)} async-done(((f32[8,2048]{1,0:T(8,128)}), f32[8,2048]{1,0:T(8,128)}) %all-reduce.2.cloned.1.call-update) | async-done | bytes 65552 | tf_op jit(solution)/shard_map/psum | solution.py:58
  90.9 0.0 copy-done.2
  90.9 1.0 multiply_reduce_fusion
  91.9 0.1 multiply_convert_fusion
  92.0 14.7 %all_gather.3 = bf16[8,2048]{1,0:T(8,128)(2,1)S(1)} all-gather(bf16[8,256]{1,0:T(8,128)(2,1)S(1)} %multiply_convert_fusion), channel_id=1, replica_groups=mesh['dp'=64,'cuts'=8] {'cuts'}, dimensions={1}, use_global_device_ids=true | all-gather | bytes 36864 | tf_op jit(solution)/shard_map/all_gather | solution.py:73
  106.6 0.2 convolution_convert_fusion.1
  106.8 0.1 reshape.81
  106.9 0.3 broadcast_in_dim.35
  107.2 0.0 copy-start.1
  107.2 46.4 %all_to_all.10 = bf16[64,2,2048]{2,1,0:T(2,128)(2,1)S(1)} all-to-all(bf16[64,2,2048]{2,1,0:T(2,128)(2,1)S(1)} %bitcast.76), channel_id=1, replica_groups=mesh['dp'=64,'cuts'=8] {'dp'}, dimensions={0} | all-to-all | bytes 1048576 | tf_op jit(solution)/shard_map/all_to_all | solution.py:78
  153.6 0.2 reshape.83
  153.8 0.0 copy-done
  153.8 0.0 copy-done.1
  153.8 1.6 fusion
  155.4 0.0 reduce-scatter.2.cloned.1.call-update
  155.4 29.1 %reduce-scatter.2.cloned.1.call-done = bf16[256,128]{0,1:T(8,128)(2,1)} async-done(((bf16[2048,128]{0,1:T(8,128)(2,1)}), bf16[256,128]{0,1:T(8,128)(2,1)}) %reduce-scatter.2.cloned.1.call-update) | async-done | bytes 65552 | tf_op jit(solution)/shard_map/reduce_scatter | solution.py:86
  184.6 0.9 reshape.84
  185.5 28.1 %all_to_all.11 = bf16[256,64,2]{0,2,1:T(2,128)(2,1)S(1)} all-to-all(bf16[256,64,2]{0,2,1:T(2,128)(2,1)S(1)} %reshape.84), channel_id=1, replica_groups=mesh['dp'=64,'cuts'=8] {'dp'}, dimensions={1} | all-to-all | bytes 131072 | tf_op jit(solution)/shard_map/all_to_all | solution.py:95
  213.5 0.1 convert_reduce_fusion
  213.6 0.8 fusion.1
  (5 shorter events, 0.1 us)
Async XLA Ops:
  6.5 147.3 %copy-start = (bf16[1,256,2048]{2,1,0:T(8,128)(2,1)S(1)}, bf16[1,256,2048]{2,1,0:T(8,128)(2,1)}, u32[]{:S(2)}) copy-start(bf16[1,256,2048]{2,1,0:T(8,128)(2,1)} %param.23) | copy-start | bytes 3145732
  6.5 84.4 %all-reduce.2.cloned.1.call-start = ((), (), s32[]{:S(2)}) async-start(), calls=%async_computation.3 | async-start | bytes 131072 | tf_op jit(solution)/shard_map/psum | solution.py:58
  7.4 0.8 copy-start.4
  7.4 2.4 %copy-start.5 = (bf16[8,64,256]{2,1,0:T(8,128)(2,1)S(1)}, bf16[8,64,256]{2,1,0:T(8,128)(2,1)}, u32[]{:S(2)}) copy-start(bf16[8,64,256]{2,1,0:T(8,128)(2,1)} %param.16) | copy-start | bytes 786436
  9.8 0.7 copy-start.3
  12.6 78.3 %copy-start.2 = (bf16[8,2048]{1,0:T(8,128)(2,1)S(1)}, bf16[8,2048]{1,0:T(8,128)(2,1)}, u32[]{:S(2)}) copy-start(bf16[8,2048]{1,0:T(8,128)(2,1)} %param.18) | copy-start | bytes 98308
  12.6 0.7 copy-start.6
  12.6 172.0 %reduce-scatter.2.cloned.1.call-start = ((), (), s32[]{:S(2)}) async-start(), calls=%async_computation.4 | async-start | bytes 589824 | tf_op jit(solution)/shard_map/reduce_scatter | solution.py:86
  107.2 46.6 %copy-start.1 = (bf16[1,2048,256]{2,1,0:T(8,128)(2,1)S(1)}, bf16[1,2048,256]{2,1,0:T(8,128)(2,1)}, u32[]{:S(2)}) copy-start(bf16[1,2048,256]{2,1,0:T(8,128)(2,1)} %param.22) | copy-start | bytes 3145732
Sparse Core Ops, SparseCore 0:
  12.7 78.1 all-reduce.1
  155.6 28.9 reduce-scatter.1
where the time goes:
time: 224 us; the launch traced here: 221 us
  waiting for transfers between devices  106 us (47%)
  blocking collectives  89.1 us (40%)
  between operations  13.5 us (6%)
  matrix products  6.02 us (3%)
  local copies, waits for them, and re-layouts  3.41 us (2%)
  other arithmetic  3.33 us (1%)
    psum x1, waiting for transfers between devices, on_device(): attn = lax.psum(partial_attn, 'cuts')  76.7 us
    all_to_all x1, blocking collectives, on_device(): lax.all_to_all(jnp.repeat(packed, GROUP, axis=0), 'dp', split_axis=0, con...  46.4 us
    reduce_scatter x1, waiting for transfers between devices, on_device(): lax.psum_scatter(lax.dot_general(lower, act, (((0,), (1,)), ((), ())), pr...  29.1 us
    all_to_all x1, blocking collectives, on_device(): lax.all_to_all(outgoing, 'dp', split_axis=1, concat_axis=1, tiled=True)  28.1 us
    all_gather x1, blocking collectives, on_device(): full_rows = lax.all_gather(normed_cols, 'cuts', axis=1, tiled=True)  14.7 us
  transfers between devices with their start and end apart: 2, of which 2 were waited for; matrix products, arithmetic and copies ran while one was open for 0% of the time, Pallas kernels for 0%

commit v1 on v0

v1 whole, which is shorter than its diff:
```python
import jax
import jax.numpy as jnp
from jax import lax
from jax.sharding import Mesh
from jax.sharding import PartitionSpec as P

HD = 128
GROUP = 4
CORES = 2
SLOTS = 2


def attend_local(queries, new_keys, new_values, key_cache, value_cache, lengths):
    count, feats = queries.shape
    heads = feats // HD
    length = key_cache.shape[1]
    scale = 1.0 / HD**0.5
    query = queries.reshape(count, heads, HD)
    kcache = key_cache.reshape(count, length, heads, HD)
    vcache = value_cache.reshape(count, length, heads, HD)
    nkey = new_keys.reshape(count, heads, HD)
    nval = new_values.reshape(count, heads, HD)
    scores = jnp.einsum("rhd,rjhd->rhj", query, kcache, preferred_element_type=jnp.float32) * scale
    keep = jnp.arange(length)[None, None, :] < lengths[:, None, None]
    scores = jnp.where(keep, scores, -1e30)
    fresh = jnp.einsum("rhd,rhd->rh", query, nkey, preferred_element_type=jnp.float32) * scale
    peak = jnp.maximum(jnp.max(scores, axis=-1), fresh)
    pcache = jnp.where(keep, jnp.exp(scores - peak[..., None]), 0.0)
    pnew = jnp.exp(fresh - peak)
    total = jnp.sum(pcache, axis=-1) + pnew
    pcache = (pcache / total[..., None]).astype(jnp.bfloat16)
    pnew = (pnew / total).astype(jnp.bfloat16)
    summed = jnp.einsum("rhj,rjhd->rhd", pcache, vcache, preferred_element_type=jnp.float32)
    summed = summed + pnew.astype(jnp.float32)[..., None] * nval.astype(jnp.float32)
    return summed.reshape(count, feats).astype(jnp.bfloat16)


def on_device(
    queries,
    new_keys,
    new_values,
    key_cache,
    value_cache,
    lengths,
    resid,
    norm_gain,
    w_out,
    experts,
    w_up,
    w_down,
):
    bf16, f32 = jnp.bfloat16, jnp.float32
    count, width_all = resid.shape
    n_z, n_x, n_y = lax.axis_size("z"), lax.axis_size("x"), lax.axis_size("y")
    width = width_all // (n_y * CORES)
    core = lax.axis_index("core")
    my_y = lax.axis_index("y")

    heads_out = attend_local(queries, new_keys, new_values, key_cache, value_cache, lengths)
    partial = jnp.dot(heads_out, w_out, preferred_element_type=f32)
    both = lax.all_gather(partial, "core", axis=0)

    ids = experts[:, 0]
    order_idx = jnp.arange(count, dtype=jnp.int32)
    earlier = (ids[:, None] == ids[None, :]) & (order_idx[:, None] > order_idx[None, :])
    slot_id = ids * SLOTS + jnp.sum(earlier.astype(jnp.int32), axis=1)
    table = jnp.arange(n_z * SLOTS, dtype=jnp.int32)[:, None] == slot_id[None, :]

    def own_half(a):
        split = a.reshape(a.shape[:-1] + (n_y, CORES, width))
        return lax.dynamic_index_in_dim(split, core, split.ndim - 2, keepdims=False)

    chip = own_half(both[0] + both[1])
    rest = own_half(resid).astype(f32)
    mine = (jnp.arange(n_y) == my_y)[None, :, None]
    chip = (chip + jnp.where(mine, rest, 0.0)).astype(bf16)
    packed = jnp.einsum("sr,ryc->syc", table.astype(bf16), chip, preferred_element_type=f32)
    packed = packed.astype(bf16).reshape(n_z, SLOTS, n_y, width).transpose(0, 2, 1, 3)
    packed = packed.reshape(n_z * n_y, SLOTS, width)
    got = lax.all_to_all(packed, ("z", "y"), split_axis=0, concat_axis=0, tiled=True)
    slots = n_z * SLOTS
    hidden = jnp.sum(got.reshape(n_z, n_y, SLOTS, width).astype(f32), axis=1).reshape(slots, width)

    spread = jnp.broadcast_to(hidden.astype(bf16)[None], (n_x * n_y, slots, width))
    plane = lax.all_to_all(spread, ("x", "y"), split_axis=0, concat_axis=0, tiled=True)
    pair = lax.all_gather(plane, "core", axis=0)
    rows = pair.reshape(CORES, n_x, n_y, slots, width).transpose(1, 3, 2, 0, 4)
    rows = rows.reshape(n_x * slots, width_all).astype(f32)
    meansq = jnp.mean(rows * rows, axis=-1)
    normed = (rows * lax.rsqrt(meansq + 1e-06)[:, None] * norm_gain[None, :]).astype(bf16)
    act = jax.nn.gelu(jnp.dot(normed, w_up[0], preferred_element_type=f32)).astype(bf16)
    piece = jnp.dot(act, w_down[0], preferred_element_type=f32).astype(bf16)
    pieces = lax.all_gather(piece, "core", axis=0)
    half = own_half(pieces).astype(f32)
    half = (half[0] + half[1]).astype(bf16)
    half = half.reshape(n_x, slots, n_y, width).transpose(0, 2, 1, 3)
    half = half.reshape(n_x * n_y, slots, width)
    parts = lax.all_to_all(half, ("x", "y"), split_axis=0, concat_axis=0, tiled=True)
    mixed = (hidden + jnp.sum(parts.astype(f32), axis=0)).astype(bf16)
    back = lax.all_to_all(
        mixed.reshape(n_z, SLOTS, width), "z", split_axis=0, concat_axis=0, tiled=True
    )
    back = back.reshape(slots, width)
    out = jnp.einsum("sr,sc->rc", table.astype(bf16), back, preferred_element_type=f32)
    return out.astype(bf16)


def solution(mesh):
    n_x = GROUP
    n_z = mesh.shape["dp"] // n_x
    n_y = mesh.shape["cuts"] // CORES
    fine = Mesh(mesh.devices.reshape(n_z, n_x, n_y, CORES), ("z", "x", "y", "core"))
    rows, cols = ("z", "x"), ("y", "core")
    placed = (
        P(rows, cols),
        P(rows, cols),
        P(rows, cols),
        P(rows, None, cols),
        P(rows, None, cols),
        P(rows),
        P(rows, None),
        P(),
        P(cols, None),
        P(rows, None),
        P(rows, None, cols),
        P(rows, cols, None),
    )
    return jax.shard_map(
        on_device, mesh=fine, in_specs=placed, out_specs=P(rows, cols), check_vma=False
    )
```

time: 224 us -> 127 us (0.57)
  waiting for transfers between devices: 106 us -> 16.4 us
  blocking collectives: 89.1 us -> 76.6 us
  starting transfers between devices: 0.04 us -> 5.06 us
  local copies, waits for them, and re-layouts: 3.41 us -> 6.98 us
    psum x1 -> x0, waiting for transfers between devices: 76.7 us -> none  [on_device(): attn = lax.psum(partial_attn, 'cuts')]
    reduce_scatter x1 -> x0, waiting for transfers between devices: 29.1 us -> none  [on_device(): lax.psum_scatter(lax.dot_general(lower, act, (((0,), (1,)), ((), ())), pr...]
    all_to_all x2 -> x3, blocking collectives: 74.5 us -> 63.2 us  [the longest x1 26.9 us: on_device(): lax.all_to_all(packed, ('z', 'y'), split_axis=0, concat_axis=0, tiled=True)]
    all_gather x0 -> x1, waiting for transfers between devices: none -> 9.15 us  [on_device(): pieces = lax.all_gather(piece, 'core', axis=0)]
    all_to_all x0 -> x1, waiting for transfers between devices: none -> 7.28 us  [on_device(): lax.all_to_all(spread, ('x', 'y'), split_axis=0, concat_axis=0, tiled=True)]
    all_to_all x0 -> x1, starting transfers between devices: none -> 5.01 us  [on_device(): lax.all_to_all(spread, ('x', 'y'), split_axis=0, concat_axis=0, tiled=True)]
    all_gather x1 -> x2, blocking collectives: 14.7 us -> 13.5 us  [the longest x1 8.42 us: on_device(): both = lax.all_gather(partial, 'core', axis=0)]
where the time goes in v1:
time: 127 us; the launch traced here: 126 us
  blocking collectives  76.6 us (60%)
  waiting for transfers between devices  16.4 us (13%)
  between operations  13.6 us (11%)
  local copies, waits for them, and re-layouts  6.98 us (5%)
  matrix products  5.52 us (4%)
  starting transfers between devices  5.06 us (4%)
  other arithmetic  1.51 us (1%)
    all_to_all x1, blocking collectives, on_device(): lax.all_to_all(packed, ('z', 'y'), split_axis=0, concat_axis=0, tiled=True)  26.9 us
    all_to_all x1, blocking collectives, on_device(): lax.all_to_all(mixed.reshape(n_z, SLOTS, width), 'z', split_axis=0, conca...  23.2 us
    all_to_all x1, blocking collectives, on_device(): lax.all_to_all(half, ('x', 'y'), split_axis=0, concat_axis=0, tiled=True)  13.1 us
    all_gather x1, waiting for transfers between devices, on_device(): pieces = lax.all_gather(piece, 'core', axis=0)  9.15 us
    all_gather x1, blocking collectives, on_device(): both = lax.all_gather(partial, 'core', axis=0)  8.42 us
    all_to_all x1, waiting for transfers between devices, on_device(): lax.all_to_all(spread, ('x', 'y'), split_axis=0, concat_axis=0, tiled=True)  7.28 us
    all_gather x1, blocking collectives, on_device(): pair = lax.all_gather(plane, 'core', axis=0)  5.04 us
    all_to_all x1, starting transfers between devices, on_device(): lax.all_to_all(spread, ('x', 'y'), split_axis=0, concat_axis=0, tiled=True)  5.01 us
  transfers between devices with their start and end apart: 2, of which 2 were waited for; matrix products, arithmetic and copies ran while one was open for 0% of the time, Pallas kernels for 0%

profile of v1, /device:TPU:1, one launch (start us, length us, event | category | flops | bytes accessed | tf_op | source)
XLA Modules:
  0.0 125.8 jit_solution(10664514927859561862)
XLA Ops:
  6.5 0.0 copy-start
  6.5 0.0 copy-start.8
  6.6 0.0 copy-start.5
  6.6 0.0 copy-start.7
  6.6 0.7 copy-done.8
  7.3 0.2 convert_reduce_fusion.2
  7.5 0.0 copy-done.9
  7.5 0.1 iota_compare_fusion
  7.6 0.0 copy-done.6
  7.6 0.0 copy-done.5
  7.6 0.1 fusion.41
  7.6 1.2 fusion.11
  8.8 0.1 fusion.46
  8.9 0.2 fusion.45
  9.1 0.1 fusion.55
  9.2 0.0 copy-done.7
  9.2 0.0 copy-start.4
  9.2 0.2 fusion.8
  9.4 0.5 copy-done.4
  9.9 1.5 %fusion.48 = f32[8,2048]{1,0:T(8,128)S(1)} fusion(bf16[256,2048]{1,0:T(8,128)(2,1)} %param.20, f32[8,2,1,128]{3,2,1,0:T(1,128)S(1)} %fusion.8, bf16[8,256]{1,0:T(8,128)(2,1)S(1)} %copy-done.4, f32[8,2]{0,1:T(2,128)S(1)} %get-tuple-element.5), kind=kOutput, calls=%fused_computation.59 | convolution fusion | flops 8396800 | bytes 1126464 | tf_op jit(solution)/shard_map/dot_general | solution.py:60
  11.4 8.4 %all-gather = f32[16,2048]{1,0:T(8,128)S(1)} all-gather(f32[8,2048]{1,0:T(8,128)S(1)} %fusion.48), channel_id=2, replica_groups=mesh['z'=16,'x'=4,'y'=4,'core'=2] {'core'}, dimensions={0}, use_global_device_ids=true | all-gather | bytes 196608 | tf_op jit(solution)/shard_map/all_gather | solution.py:61
  19.8 0.7 copy-done.2
  20.6 0.3 convolution_convert_fusion.1
  21.0 26.9 %all_to_all.20 = bf16[64,2,256]{2,1,0:T(2,128)(2,1)S(1)} all-to-all(bf16[64,2,256]{2,1,0:T(2,128)(2,1)S(1)} %bitcast.105), channel_id=1, replica_groups=mesh['z'=16,'x'=4,'y'=4,'core'=2] {'z','y'}, dimensions={0} | all-to-all | bytes 131072 | tf_op jit(solution)/shard_map/all_to_all | solution.py:80
  47.9 0.1 convert_reduce_fusion.1
  48.0 0.7 broadcast_in_dim.53
  48.7 5.0 %all-to-all-start.1 = ((bf16[16,32,256]{2,1,0:T(8,128)(2,1)}), bf16[16,32,256]{2,1,0:T(8,128)(2,1)S(1)}, u32[]{:S(2)}, u32[]{:S(2)}) async-start(bf16[16,32,256]{2,1,0:T(8,128)(2,1)} %broadcast_in_dim.53), calls=%async_computation.1 | async-start | bytes 524288 | tf_op jit(solution)/shard_map/all_to_all | solution.py:85
  53.7 0.0 all-gather.5.cloned.1.call-start
  53.7 0.0 copy-done.3
  53.8 7.3 %all-to-all-done.1 = bf16[16,32,256]{2,1,0:T(8,128)(2,1)S(1)} async-done(((bf16[16,32,256]{2,1,0:T(8,128)(2,1)}), bf16[16,32,256]{2,1,0:T(8,128)(2,1)S(1)}, u32[]{:S(2)}, u32[]{:S(2)}) %all-to-all-start.1) | async-done | bytes 262176 | tf_op jit(solution)/shard_map/all_to_all | solution.py:85
  61.1 5.0 %all-gather.1 = bf16[32,32,256]{2,1,0:T(8,128)(2,1)S(1)} all-gather(bf16[16,32,256]{2,1,0:T(8,128)(2,1)S(1)} %all-to-all-done.1), channel_id=3, replica_groups=mesh['z'=16,'x'=4,'y'=4,'core'=2] {'core'}, dimensions={0}, use_global_device_ids=true | all-gather | bytes 786432 | tf_op jit(solution)/shard_map/all_gather | solution.py:86
  66.1 0.2 fusion
  66.3 0.2 fusion.3
  66.5 0.0 copy-start.1
  66.5 0.5 copy.41
  67.1 0.4 convert_element_type.116
  67.5 0.0 copy-done
  67.5 0.3 copy-done.1
  67.7 1.6 %convolution_convert_fusion = bf16[128,2048]{1,0:T(8,128)(2,1)} fusion(bf16[1,256,2048]{2,1,0:T(8,128)(2,1)S(1)} %copy-done, bf16[128,2048]{1,0:T(8,128)(2,1)S(1)} %convert_element_type.116, bf16[1,2048,256]{2,1,0:T(8,128)(2,1)S(1)} %copy-done.1), kind=kOutput, calls=%fused_computation | convolution fusion | flops 268992512 | bytes 3145728 | tf_op jit(solution)/shard_map/dot_general | solution.py:92
  69.3 0.0 all-gather.5.cloned.1.call-update
  69.4 9.2 %all-gather.5.cloned.1.call-done = bf16[256,2048]{1,0:T(8,128)(2,1)} async-done(((bf16[128,2048]{1,0:T(8,128)(2,1)}), bf16[256,2048]{1,0:T(8,128)(2,1)}) %all-gather.5.cloned.1.call-update) | async-done | bytes 1048592 | tf_op jit(solution)/shard_map/all_gather | solution.py:93
  78.5 1.8 %reshape.132 = bf16[2,128,4,2,256]{4,3,2,1,0:T(2,128)(2,1)S(1)} reshape(bf16[256,2048]{1,0:T(8,128)(2,1)} %all-gather.5.cloned.1.call-done) | data formatting | bytes 2097152 | tf_op jit(solution)/shard_map/reshape | solution.py:70
  80.4 1.1 constant_dynamic-slice_fusion
  81.5 0.2 copy_convert_fusion
  81.7 0.1 fusion.7
  81.7 13.1 %all_to_all.21 = bf16[16,32,256]{2,1,0:T(8,128)(2,1)S(1)} all-to-all(bf16[16,32,256]{2,1,0:T(8,128)(2,1)S(1)} %bitcast.104), channel_id=1, replica_groups=mesh['z'=16,'x'=4,'y'=4,'core'=2] {'x','y'}, dimensions={0} | all-to-all | bytes 524288 | tf_op jit(solution)/shard_map/all_to_all | solution.py:98
  94.9 23.2 %all_to_all.22 = bf16[16,2,256]{2,1,0:T(2,128)(2,1)S(1)} all-to-all(bf16[16,2,256]{2,1,0:T(2,128)(2,1)S(1)} %add_convert_fusion), channel_id=1, replica_groups=mesh['z'=16,'x'=4,'y'=4,'core'=2] {'z'}, dimensions={0} | all-to-all | bytes 32768 | tf_op jit(solution)/shard_map/all_to_all | solution.py:100
  118.1 0.8 convolution_convert_fusion.2
  (21 shorter events, 0.3 us)
Async XLA Ops:
  6.5 60.9 %copy-start = (bf16[1,256,2048]{2,1,0:T(8,128)(2,1)S(1)}, bf16[1,256,2048]{2,1,0:T(8,128)(2,1)}, u32[]{:S(2)}) copy-start(bf16[1,256,2048]{2,1,0:T(8,128)(2,1)} %param.23) | copy-start | bytes 3145732
  6.5 0.7 copy-start.8
  6.5 0.9 copy-start.9
  6.5 1.0 copy-start.6
  6.6 1.0 copy-start.5
  6.6 2.6 %copy-start.7 = (bf16[8,64,256]{2,1,0:T(8,128)(2,1)S(1)}, bf16[8,64,256]{2,1,0:T(8,128)(2,1)}, u32[]{:S(2)}) copy-start(bf16[8,64,256]{2,1,0:T(8,128)(2,1)} %param.16) | copy-start | bytes 786436
  9.2 0.7 copy-start.4
  19.8 0.8 copy-start.2
  48.7 5.1 %copy-start.3 = (f32[2048]{0:T(1024)S(1)}, f32[2048]{0:T(1024)}, u32[]{:S(2)}) copy-start(f32[2048]{0:T(1024)} %param.19) | copy-start | bytes 24580
  48.7 12.4 %all-to-all-start.1 = ((bf16[16,32,256]{2,1,0:T(8,128)(2,1)}), bf16[16,32,256]{2,1,0:T(8,128)(2,1)S(1)}, u32[]{:S(2)}, u32[]{:S(2)}) async-start(bf16[16,32,256]{2,1,0:T(8,128)(2,1)} %broadcast_in_dim.53), calls=%async_computation.1 | async-start | bytes 524288 | tf_op jit(solution)/shard_map/all_to_all | solution.py:85
  53.7 24.8 %all-gather.5.cloned.1.call-start = ((), (), s32[]{:S(2)}) async-start(), calls=%async_computation.4 | async-start | bytes 1572864 | tf_op jit(solution)/shard_map/all_gather | solution.py:93
  66.5 1.2 copy-start.1
Sparse Core Ops, SparseCore 0:
  69.5 8.9 all-gather.4

commit v2 on v1

v2 whole, which is shorter than its diff:
```python
import functools

import jax
import jax.numpy as jnp
from jax import lax
from jax.experimental import pallas as pl
from jax.experimental.pallas import tpu as pltpu
from jax.sharding import Mesh
from jax.sharding import PartitionSpec as P

HD = 128
GROUP = 4
CORES = 2
SLOTS = 2


def attend_kernel(
    n_y,
    queries,
    new_keys,
    new_values,
    key_cache,
    value_cache,
    lengths,
    resid,
    w_out,
    keep,
    give,
    weights,
    sem,
):
    f32, bf16 = jnp.float32, jnp.bfloat16
    core, my_y = lax.axis_index("core"), lax.axis_index("y")
    copy = pltpu.make_async_copy(w_out, weights, sem)
    copy.start()
    count, feats = queries.shape
    spots = key_cache.shape[0]
    length = spots // count
    scale = 1.0 / HD**0.5
    row = lax.broadcasted_iota(jnp.int32, (count, spots), 0)
    spot = lax.broadcasted_iota(jnp.int32, (count, spots), 1)
    limit = jnp.zeros((count, spots), jnp.int32)
    for r in range(count):
        limit = jnp.where(row == r, r * length + lengths[r], limit)
    valid = (spot >= row * length) & (spot < limit)
    heads = []
    for h in range(feats // HD):
        cols = slice(h * HD, (h + 1) * HD)
        query = queries[:, cols]
        scores = lax.dot_general(
            query, key_cache[:, cols], (((1,), (1,)), ((), ())), preferred_element_type=f32
        )
        scores = jnp.where(valid, scores * scale, -1e30)
        fresh = query.astype(f32) * new_keys[:, cols].astype(f32)
        fresh = jnp.sum(fresh, axis=-1, keepdims=True) * scale
        peak = jnp.maximum(jnp.max(scores, axis=-1, keepdims=True), fresh)
        pcache = jnp.where(valid, jnp.exp(scores - peak), 0.0)
        pnew = jnp.exp(fresh - peak)
        total = jnp.sum(pcache, axis=-1, keepdims=True) + pnew
        pcache = (pcache / total).astype(bf16)
        pnew = (pnew / total).astype(bf16).astype(f32)
        summed = jnp.dot(pcache, value_cache[:, cols], preferred_element_type=f32)
        summed = summed + pnew * new_values[:, cols].astype(f32)
        heads.append(summed.astype(bf16))
    heads_out = jnp.concatenate(heads, axis=1)
    copy.wait()
    width = weights.shape[1] // (n_y * CORES)
    for y in range(n_y):
        pair = []
        for c in range(CORES):
            cols = pl.ds((y * CORES + c) * width, width)
            pair.append(jnp.dot(heads_out, weights[:, cols], preferred_element_type=f32))
        low = resid[:, pl.ds(y * CORES * width, width)].astype(f32)
        high = resid[:, pl.ds((y * CORES + 1) * width, width)].astype(f32)
        rest = jnp.where(my_y == y, jnp.where(core == 0, low, high), 0.0)
        keep[:, pl.ds(y * width, width)] = jnp.where(core == 0, pair[0], pair[1]) + rest
        give[:, pl.ds(y * width, width)] = jnp.where(core == 0, pair[1], pair[0])


def attend(
    n_y, queries, new_keys, new_values, key_cache, value_cache, lengths, resid, w_out
):
    count, feats = queries.shape
    spots = count * key_cache.shape[1]
    vmem, smem = pl.BlockSpec(memory_space=pltpu.VMEM), pl.BlockSpec(memory_space=pltpu.SMEM)
    half = jax.ShapeDtypeStruct((count, w_out.shape[1] // CORES), jnp.float32)
    return pl.pallas_call(
        functools.partial(attend_kernel, n_y),
        out_shape=(half, half),
        in_specs=[vmem] * 5 + [smem, vmem, pl.BlockSpec(memory_space=pl.ANY)],
        out_specs=(vmem, vmem),
        scratch_shapes=[pltpu.VMEM(w_out.shape, w_out.dtype), pltpu.SemaphoreType.DMA],
        name="attend",
    )(
        queries,
        new_keys,
        new_values,
        key_cache.reshape(spots, feats),
        value_cache.reshape(spots, feats),
        lengths,
        resid,
        w_out,
    )


def expert_kernel(n_x, n_y, pair, gain, w_up, w_down, keep, give, up, down, sems):
    f32, bf16 = jnp.float32, jnp.bfloat16
    core = lax.axis_index("core")
    copies = [
        pltpu.make_async_copy(w_up, up, sems.at[0]),
        pltpu.make_async_copy(w_down, down, sems.at[1]),
    ]
    for copy in copies:
        copy.start()
    slots, width = pair.shape[2:]
    width_all = n_y * CORES * width
    blocks = []
    squares = jnp.zeros((n_x * slots, 1), f32)
    for y in range(n_y):
        for c in range(CORES):
            block = [pair[c, x * n_y + y].astype(f32) for x in range(n_x)]
            block = jnp.concatenate(block, axis=0)
            squares = squares + jnp.sum(block * block, axis=-1, keepdims=True)
            blocks.append(block)
    inverse = lax.rsqrt(squares * (1.0 / width_all) + 1e-06)
    normed = [
        (block * inverse * gain[:, pl.ds(i * width, width)]).astype(bf16)
        for i, block in enumerate(blocks)
    ]
    copies[0].wait()
    units = jnp.zeros((n_x * slots, up.shape[1]), f32)
    for i, block in enumerate(normed):
        units = units + jnp.dot(block, up[pl.ds(i * width, width), :], preferred_element_type=f32)
    act = jax.nn.gelu(units).astype(bf16)
    copies[1].wait()
    for y in range(n_y):
        both = []
        for c in range(CORES):
            cols = pl.ds((y * CORES + c) * width, width)
            both.append(jnp.dot(act, down[:, cols], preferred_element_type=f32))
        own = jnp.where(core == 0, both[0], both[1])
        other = jnp.where(core == 0, both[1], both[0]).astype(bf16)
        for x in range(n_x):
            keep[x * n_y + y] = own[x * slots : (x + 1) * slots]
            give[x * n_y + y] = other[x * slots : (x + 1) * slots]


def run_expert(n_x, n_y, pair, norm_gain, w_up, w_down):
    vmem, anywhere = pl.BlockSpec(memory_space=pltpu.VMEM), pl.BlockSpec(memory_space=pl.ANY)
    return pl.pallas_call(
        functools.partial(expert_kernel, n_x, n_y),
        out_shape=(
            jax.ShapeDtypeStruct(pair.shape[1:], jnp.float32),
            jax.ShapeDtypeStruct(pair.shape[1:], jnp.bfloat16),
        ),
        in_specs=[vmem, vmem, anywhere, anywhere],
        out_specs=(vmem, vmem),
        scratch_shapes=[
            pltpu.VMEM(w_up.shape, w_up.dtype),
            pltpu.VMEM(w_down.shape, w_down.dtype),
            pltpu.SemaphoreType.DMA((2,)),
        ],
        name="expert",
    )(pair, norm_gain[None, :], w_up, w_down)


def on_device(
    queries,
    new_keys,
    new_values,
    key_cache,
    value_cache,
    lengths,
    resid,
    norm_gain,
    w_out,
    experts,
    w_up,
    w_down,
):
    bf16, f32 = jnp.bfloat16, jnp.float32
    count, width_all = resid.shape
    n_z, n_x, n_y = lax.axis_size("z"), lax.axis_size("x"), lax.axis_size("y")
    width = width_all // (n_y * CORES)
    core = lax.axis_index("core")
    my_y = lax.axis_index("y")

    keep, give = attend(
        n_y, queries, new_keys, new_values, key_cache, value_cache, lengths, resid, w_out
    )
    given = lax.all_gather(give, "core", axis=0)

    ids = experts[:, 0]
    order_idx = jnp.arange(count, dtype=jnp.int32)
    earlier = (ids[:, None] == ids[None, :]) & (order_idx[:, None] > order_idx[None, :])
    slot_id = ids * SLOTS + jnp.sum(earlier.astype(jnp.int32), axis=1)
    table = jnp.arange(n_z * SLOTS, dtype=jnp.int32)[:, None] == slot_id[None, :]

    chip = keep + lax.dynamic_index_in_dim(given, 1 - core, 0, keepdims=False)
    chip = chip.astype(bf16).reshape(count, n_y, width)
    packed = jnp.einsum("sr,ryc->syc", table.astype(bf16), chip, preferred_element_type=f32)
    packed = packed.astype(bf16).reshape(n_z, SLOTS, n_y, width).transpose(0, 2, 1, 3)
    packed = packed.reshape(n_z * n_y, SLOTS, width)
    got = lax.all_to_all(packed, ("z", "y"), split_axis=0, concat_axis=0, tiled=True)
    slots = n_z * SLOTS
    hidden = jnp.sum(got.reshape(n_z, n_y, SLOTS, width).astype(f32), axis=1).reshape(slots, width)

    spread = jnp.broadcast_to(hidden.astype(bf16)[None], (n_x * n_y, slots, width))
    plane = lax.all_to_all(spread, ("x", "y"), split_axis=0, concat_axis=0, tiled=True)
    pair = lax.all_gather(plane, "core", axis=0)
    keep, give = run_expert(n_x, n_y, pair, norm_gain, w_up[0], w_down[0])
    given = lax.all_gather(give, "core", axis=0)
    half = keep + lax.dynamic_index_in_dim(given, 1 - core, 0, keepdims=False).astype(f32)
    half = half.astype(bf16)
    parts = lax.all_to_all(half, ("x", "y"), split_axis=0, concat_axis=0, tiled=True)
    mixed = (hidden + jnp.sum(parts.astype(f32), axis=0)).astype(bf16)
    back = lax.all_to_all(
        mixed.reshape(n_z, SLOTS, width), "z", split_axis=0, concat_axis=0, tiled=True
    )
    back = back.reshape(slots, width)
    out = jnp.einsum("sr,sc->rc", table.astype(bf16), back, preferred_element_type=f32)
    return out.astype(bf16)


def solution(mesh):
    n_x = GROUP
    n_z = mesh.shape["dp"] // n_x
    n_y = mesh.shape["cuts"] // CORES
    fine = Mesh(mesh.devices.reshape(n_z, n_x, n_y, CORES), ("z", "x", "y", "core"))
    rows, cols = ("z", "x"), ("y", "core")
    placed = (
        P(rows, cols),
        P(rows, cols),
        P(rows, cols),
        P(rows, None, cols),
        P(rows, None, cols),
        P(rows),
        P(rows, None),
        P(),
        P(cols, None),
        P(rows, None),
        P(rows, None, cols),
        P(rows, cols, None),
    )
    return jax.shard_map(
        on_device, mesh=fine, in_specs=placed, out_specs=P(rows, cols), check_vma=False
    )
```

time: 127 us -> 90.3 us (0.71)
  waiting for transfers between devices: 16.4 us -> 0 us
  between operations: 13.6 us -> 0.1 us
  Pallas kernels: 0 us -> 7.26 us
  local copies, waits for them, and re-layouts: 6.98 us -> 0.82 us
  starting transfers between devices: 5.06 us -> 0 us
  matrix products: 5.52 us -> 1.05 us
  blocking collectives: 76.6 us -> 79.8 us
    all_to_all x0 -> x1, blocking collectives: none -> 12 us  [on_device(): lax.all_to_all(spread, ('x', 'y'), split_axis=0, concat_axis=0, tiled=True)]
    all_to_all x1, blocking collectives: 23.2 us -> 13.8 us  [on_device(): lax.all_to_all(mixed.reshape(n_z, SLOTS, width), 'z', split_axis=0, conca...]
    all_gather x1 -> x0, waiting for transfers between devices: 9.15 us -> none  [on_device(): pieces = lax.all_gather(piece, 'core', axis=0)]
    all_to_all x1 -> x0, waiting for transfers between devices: 7.28 us -> none  [on_device(): lax.all_to_all(spread, ('x', 'y'), split_axis=0, concat_axis=0, tiled=True)]
    pallas_call x0 -> x2, Pallas kernels: none -> 7.26 us  [the longest x1 4.05 us: run_expert(): pl.pallas_call(functools.partial(expert_kernel, n_x, n_y), out_shape=(jax...]
    all_to_all x1 -> x0, starting transfers between devices: 5.01 us -> none  [on_device(): lax.all_to_all(spread, ('x', 'y'), split_axis=0, concat_axis=0, tiled=True)]
    dot_general x4 -> x0, matrix products: 4.47 us -> none  [the longest x1 1.61 us: on_device(): piece = jnp.dot(act, w_down[0], preferred_element_type=f32).astype(bf16)]
    all_gather x1 -> x2, blocking collectives: 8.42 us -> 11.1 us  [on_device(): given = lax.all_gather(give, 'core', axis=0)]
  transfers between devices with their start and end apart: 2 -> 0, of which waited for: 2 -> 0; matrix products, arithmetic and copies ran while one was open for 0% -> 0% of each run, Pallas kernels for 0% -> 0%
where the time goes in v2:
time: 90.3 us; the launch traced here: 89.4 us
  blocking collectives  79.8 us (88%)
  Pallas kernels  7.26 us (8%)
  matrix products  1.05 us (1%)
    all_to_all x1, blocking collectives, on_device(): lax.all_to_all(packed, ('z', 'y'), split_axis=0, concat_axis=0, tiled=True)  26.9 us
    all_to_all x1, blocking collectives, on_device(): lax.all_to_all(mixed.reshape(n_z, SLOTS, width), 'z', split_axis=0, conca...  13.8 us
    all_to_all x1, blocking collectives, on_device(): lax.all_to_all(spread, ('x', 'y'), split_axis=0, concat_axis=0, tiled=True)  12 us
    all_gather x2, blocking collectives, on_device(): given = lax.all_gather(give, 'core', axis=0)  11.1 us
    all_to_all x1, blocking collectives, on_device(): lax.all_to_all(half, ('x', 'y'), split_axis=0, concat_axis=0, tiled=True)  10.7 us
    all_gather x1, blocking collectives, on_device(): pair = lax.all_gather(plane, 'core', axis=0)  5.17 us
    pallas_call x1, Pallas kernels, run_expert(): pl.pallas_call(functools.partial(expert_kernel, n_x, n_y), out_shape=(jax...  4.05 us
    pallas_call x1, Pallas kernels, attend(): pl.pallas_call(functools.partial(attend_kernel, n_y), out_shape=(half, ha...  3.21 us

profile of v2, /device:TPU:1, one launch (start us, length us, event | category | flops | bytes accessed | tf_op | source)
XLA Modules:
  0.0 89.4 jit_solution(15073232320347957676)
XLA Ops:
  0.0 0.0 copy-start.2
  0.0 0.7 copy-done.2
  0.7 0.2 convert_reduce_fusion.2
  0.8 3.2 %attend.1 = (f32[8,1024]{1,0:T(8,128)}, f32[8,1024]{1,0:T(8,128)}) custom-call(bf16[8,256]{1,0:T(8,128)(2,1)} %queries.1, bf16[8,256]{1,0:T(8,128)(2,1)} %new_keys.1, bf16[8,256]{1,0:T(8,128)(2,1)} %new_values.1, bf16[512,256]{1,0:T(8,128)(2,1)} %bitcast.36, bf16[512,256]{1,0:T(8,128)(2,1)} %bitcast.37, s32[8]{0:T(128)} %lengths.1, bf16[8,2048]{1,0:T(8,128)(2,1)} %resid.1, ...), custom_call_target="tpu_custom_call" | custom-call | tf_op jit(solution)/shard_map/attend/pallas_call | solution.py:87
  4.1 0.0 copy-start.1
  4.1 8.6 %all-gather = f32[16,1024]{1,0:T(8,128)S(1)} all-gather(f32[8,1024]{1,0:T(8,128)} %get-tuple-element.10), channel_id=2, replica_groups=mesh['z'=16,'x'=4,'y'=4,'core'=2] {'core'}, dimensions={0}, use_global_device_ids=true | all-gather | bytes 98304 | tf_op jit(solution)/shard_map/all_gather | solution.py:191
  12.7 0.0 copy-done.1
  12.7 0.3 convolution_convert_fusion
  13.1 26.9 %all_to_all.20 = bf16[64,2,256]{2,1,0:T(2,128)(2,1)S(1)} all-to-all(bf16[64,2,256]{2,1,0:T(2,128)(2,1)S(1)} %bitcast.35), channel_id=1, replica_groups=mesh['z'=16,'x'=4,'y'=4,'core'=2] {'z','y'}, dimensions={0} | all-to-all | bytes 131072 | tf_op jit(solution)/shard_map/all_to_all | solution.py:204
  39.9 0.1 convert_reduce_fusion.1
  40.1 12.0 %all_to_all.21 = bf16[16,32,256]{2,1,0:T(8,128)(2,1)S(1)} all-to-all(bf16[16,32,256]{2,1,0:T(8,128)(2,1)S(1)} %broadcast_in_dim.4), channel_id=1, replica_groups=mesh['z'=16,'x'=4,'y'=4,'core'=2] {'x','y'}, dimensions={0} | all-to-all | bytes 524288 | tf_op jit(solution)/shard_map/all_to_all | solution.py:209
  52.1 5.2 %all-gather.1 = bf16[32,32,256]{2,1,0:T(8,128)(2,1)} all-gather(bf16[16,32,256]{2,1,0:T(8,128)(2,1)S(1)} %all_to_all.21), channel_id=3, replica_groups=mesh['z'=16,'x'=4,'y'=4,'core'=2] {'core'}, dimensions={0}, use_global_device_ids=true | all-gather | bytes 786432 | tf_op jit(solution)/shard_map/all_gather | solution.py:210
  57.3 4.0 %expert.1 = (f32[16,32,256]{2,1,0:T(8,128)}, bf16[16,32,256]{2,1,0:T(8,128)(2,1)}) custom-call(bf16[2,16,32,256]{3,2,1,0:T(8,128)(2,1)} %bitcast.31, f32[1,2048]{1,0:T(1,128)} %bitcast.40, bf16[2048,256]{1,0:T(8,128)(2,1)} %bitcast.33, bf16[256,2048]{1,0:T(8,128)(2,1)} %bitcast.34), custom_call_target="tpu_custom_call" | custom-call | tf_op jit(solution)/shard_map/expert/pallas_call | solution.py:150
  61.3 0.0 copy-start
  61.4 2.5 %all-gather.2 = bf16[32,32,256]{2,1,0:T(8,128)(2,1)S(1)} all-gather(bf16[16,32,256]{2,1,0:T(8,128)(2,1)} %get-tuple-element.12), channel_id=4, replica_groups=mesh['z'=16,'x'=4,'y'=4,'core'=2] {'core'}, dimensions={0}, use_global_device_ids=true | all-gather | bytes 786432 | tf_op jit(solution)/shard_map/all_gather | solution.py:212
  63.9 0.0 copy-done
  63.9 0.1 fusion
  64.0 10.7 %all_to_all.22 = bf16[16,32,256]{2,1,0:T(8,128)(2,1)S(1)} all-to-all(bf16[16,32,256]{2,1,0:T(8,128)(2,1)S(1)} %fusion), channel_id=1, replica_groups=mesh['z'=16,'x'=4,'y'=4,'core'=2] {'x','y'}, dimensions={0} | all-to-all | bytes 524288 | tf_op jit(solution)/shard_map/all_to_all | solution.py:215
  74.8 13.8 %all_to_all.23 = bf16[16,2,256]{2,1,0:T(2,128)(2,1)S(1)} all-to-all(bf16[16,2,256]{2,1,0:T(2,128)(2,1)S(1)} %add_convert_fusion), channel_id=1, replica_groups=mesh['z'=16,'x'=4,'y'=4,'core'=2] {'z'}, dimensions={0} | all-to-all | bytes 32768 | tf_op jit(solution)/shard_map/all_to_all | solution.py:217
  88.6 0.8 convolution_convert_fusion.1
  (11 shorter events, 0.2 us)
Async XLA Ops:
  0.0 0.7 copy-start.2
  4.1 8.6 %copy-start.1 = (f32[8,1024]{1,0:T(8,128)S(1)}, f32[8,1024]{1,0:T(8,128)}, u32[]{:S(2)}) copy-start(f32[8,1024]{1,0:T(8,128)} %get-tuple-element.9) | copy-start | bytes 98308
  61.3 2.5 %copy-start = (f32[16,32,256]{2,1,0:T(8,128)S(1)}, f32[16,32,256]{2,1,0:T(8,128)}, u32[]{:S(2)}) copy-start(f32[16,32,256]{2,1,0:T(8,128)} %get-tuple-element.11) | copy-start | bytes 1572868

commit v3 on v2

v3 whole, which is shorter than its diff:
```python
import functools

import jax
import jax.numpy as jnp
from jax import lax
from jax.experimental import pallas as pl
from jax.experimental.pallas import tpu as pltpu
from jax.sharding import Mesh
from jax.sharding import PartitionSpec as P

HD = 128
GROUP = 4
CORES = 2
SLOTS = 2


def in_vmem(shape, dtype):
    return pltpu.VMEM(shape, dtype)


def attend_kernel(n_y, *refs):
    f32, bf16 = jnp.float32, jnp.bfloat16
    sources, (keep, give, table), held, sems = refs[:9], refs[9:12], refs[12:21], refs[21]
    core, my_y = lax.axis_index("core"), lax.axis_index("y")
    copies = [
        pltpu.make_async_copy(source, target, sems.at[i])
        for i, (source, target) in enumerate(zip(sources, held))
    ]
    for copy in copies:
        copy.start()
    lengths, ids, queries, key_cache, new_keys, value_cache, new_values, w_out, resid = held
    count, feats = queries.shape
    spots = key_cache.shape[0]
    length = spots // count
    scale = 1.0 / HD**0.5
    for copy in copies[:2]:
        copy.wait()
    row = lax.broadcasted_iota(jnp.int32, (count, spots), 0)
    spot = lax.broadcasted_iota(jnp.int32, (count, spots), 1)
    limit = jnp.zeros((count, spots), jnp.int32)
    for r in range(count):
        limit = jnp.where(row == r, r * length + lengths[r], limit)
    valid = (spot >= row * length) & (spot < limit)
    slot = lax.broadcasted_iota(jnp.int32, table.shape, 0)
    name = lax.broadcasted_iota(jnp.int32, table.shape, 1)
    hot = jnp.zeros(table.shape, f32)
    for r in range(count):
        place = ids[r] * SLOTS
        for q in range(r):
            place = place + (ids[q] == ids[r]).astype(jnp.int32)
        hot = jnp.where((name == r) & (slot == place), 1.0, hot)
    table[...] = hot.astype(bf16)
    for copy in copies[2:5]:
        copy.wait()
    probs = []
    for h in range(feats // HD):
        cols = slice(h * HD, (h + 1) * HD)
        query = queries[:, cols]
        scores = lax.dot_general(
            query, key_cache[:, cols], (((1,), (1,)), ((), ())), preferred_element_type=f32
        )
        scores = jnp.where(valid, scores * scale, -1e30)
        fresh = query.astype(f32) * new_keys[:, cols].astype(f32)
        fresh = jnp.sum(fresh, axis=-1, keepdims=True) * scale
        peak = jnp.maximum(jnp.max(scores, axis=-1, keepdims=True), fresh)
        pcache = jnp.where(valid, jnp.exp(scores - peak), 0.0)
        pnew = jnp.exp(fresh - peak)
        total = jnp.sum(pcache, axis=-1, keepdims=True) + pnew
        probs.append(((pcache / total).astype(bf16), (pnew / total).astype(bf16).astype(f32)))
    for copy in copies[5:7]:
        copy.wait()
    heads = []
    for h, (pcache, pnew) in enumerate(probs):
        cols = slice(h * HD, (h + 1) * HD)
        summed = jnp.dot(pcache, value_cache[:, cols], preferred_element_type=f32)
        summed = summed + pnew * new_values[:, cols].astype(f32)
        heads.append(summed.astype(bf16))
    heads_out = jnp.concatenate(heads, axis=1)
    for copy in copies[7:]:
        copy.wait()
    width = w_out.shape[1] // (n_y * CORES)
    for y in range(n_y):
        pair = []
        for c in range(CORES):
            cols = pl.ds((y * CORES + c) * width, width)
            pair.append(jnp.dot(heads_out, w_out[:, cols], preferred_element_type=f32))
        low = resid[:, pl.ds(y * CORES * width, width)].astype(f32)
        high = resid[:, pl.ds((y * CORES + 1) * width, width)].astype(f32)
        rest = jnp.where(my_y == y, jnp.where(core == 0, low, high), 0.0)
        keep[:, pl.ds(y * width, width)] = jnp.where(core == 0, pair[0], pair[1]) + rest
        give[:, pl.ds(y * width, width)] = jnp.where(core == 0, pair[1], pair[0])


def attend(
    n_y,
    slots,
    queries,
    new_keys,
    new_values,
    key_cache,
    value_cache,
    lengths,
    resid,
    w_out,
    ids,
):
    count, feats = queries.shape
    spots = count * key_cache.shape[1]
    args = (
        lengths,
        ids,
        queries,
        key_cache.reshape(spots, feats),
        new_keys,
        value_cache.reshape(spots, feats),
        new_values,
        w_out,
        resid,
    )
    half = in_vmem((count, w_out.shape[1] // CORES), jnp.float32)
    vmem, anywhere = pl.BlockSpec(memory_space=pltpu.VMEM), pl.BlockSpec(memory_space=pl.ANY)
    spaces = [pltpu.SMEM] * 2 + [pltpu.VMEM] * 7
    return pl.pallas_call(
        functools.partial(attend_kernel, n_y),
        out_shape=(half, half, in_vmem((slots, count), jnp.bfloat16)),
        in_specs=[anywhere] * len(args),
        out_specs=(vmem,) * 3,
        scratch_shapes=[space(arg.shape, arg.dtype) for space, arg in zip(spaces, args)]
        + [pltpu.SemaphoreType.DMA((len(args),))],
        name="attend",
    )(*args)


def expert_kernel(n_x, n_y, pair, gain, up, down, keep, give, normed):
    f32, bf16 = jnp.float32, jnp.bfloat16
    core = lax.axis_index("core")
    slots, width = pair.shape[2:]
    width_all = n_y * CORES * width
    blocks = [(y, c) for y in range(n_y) for c in range(CORES)]
    for x in range(n_x):
        squares = jnp.zeros((slots, width), f32)
        for y, c in blocks:
            block = pair[c, x * n_y + y].astype(f32)
            squares = squares + block * block
        meansq = jnp.sum(squares, axis=-1, keepdims=True) * (1.0 / width_all)
        inverse = lax.rsqrt(meansq + 1e-06)
        for y, c in blocks:
            cols = pl.ds((y * CORES + c) * width, width)
            block = pair[c, x * n_y + y].astype(f32) * inverse * gain[:, cols]
            normed[pl.ds(x * slots, slots), cols] = block.astype(bf16)
    units = jnp.dot(normed[...], up[...], preferred_element_type=f32)
    act = jax.nn.gelu(units).astype(bf16)
    for y in range(n_y):
        both = []
        for c in range(CORES):
            cols = pl.ds((y * CORES + c) * width, width)
            both.append(jnp.dot(act, down[:, cols], preferred_element_type=f32))
        own = jnp.where(core == 0, both[0], both[1])
        other = jnp.where(core == 0, both[1], both[0]).astype(bf16)
        for x in range(n_x):
            keep[x * n_y + y] = own[x * slots : (x + 1) * slots]
            give[x * n_y + y] = other[x * slots : (x + 1) * slots]


def run_expert(n_x, n_y, pair, norm_gain, w_up, w_down):
    vmem = pl.BlockSpec(memory_space=pltpu.VMEM)
    args = [
        pltpu.with_memory_space_constraint(arg, pltpu.VMEM)
        for arg in (pair, norm_gain[None, :], w_up, w_down)
    ]
    return pl.pallas_call(
        functools.partial(expert_kernel, n_x, n_y),
        out_shape=(
            in_vmem(pair.shape[1:], jnp.float32),
            in_vmem(pair.shape[1:], jnp.bfloat16),
        ),
        in_specs=[vmem] * 4,
        out_specs=(vmem, vmem),
        scratch_shapes=[pltpu.VMEM((n_x * pair.shape[2], w_up.shape[0]), jnp.bfloat16)],
        name="expert",
    )(*args)


def on_device(
    queries,
    new_keys,
    new_values,
    key_cache,
    value_cache,
    lengths,
    resid,
    norm_gain,
    w_out,
    experts,
    w_up,
    w_down,
):
    bf16, f32 = jnp.bfloat16, jnp.float32
    count, width_all = resid.shape
    n_z, n_x, n_y = lax.axis_size("z"), lax.axis_size("x"), lax.axis_size("y")
    width = width_all // (n_y * CORES)
    core = lax.axis_index("core")

    slots = n_z * SLOTS
    keep, give, table = attend(
        n_y,
        slots,
        queries,
        new_keys,
        new_values,
        key_cache,
        value_cache,
        lengths,
        resid,
        w_out,
        experts[:, 0],
    )
    given = lax.all_gather(give, "core", axis=0)
    chip = keep + lax.dynamic_index_in_dim(given, 1 - core, 0, keepdims=False)
    chip = chip.astype(bf16).reshape(count, n_y, width)
    packed = jnp.einsum("sr,ryc->syc", table, chip, preferred_element_type=f32)
    packed = packed.astype(bf16).reshape(n_z, SLOTS, n_y, width).transpose(0, 2, 1, 3)
    packed = packed.reshape(n_z * n_y, SLOTS, width)
    got = lax.all_to_all(packed, ("z", "y"), split_axis=0, concat_axis=0, tiled=True)
    hidden = jnp.sum(got.reshape(n_z, n_y, SLOTS, width).astype(f32), axis=1).reshape(slots, width)

    spread = jnp.broadcast_to(hidden.astype(bf16)[None], (n_x * n_y, slots, width))
    plane = lax.all_to_all(spread, ("x", "y"), split_axis=0, concat_axis=0, tiled=True)
    pair = lax.all_gather(plane, "core", axis=0)
    keep, give = run_expert(n_x, n_y, pair, norm_gain, w_up[0], w_down[0])
    given = lax.all_gather(give, "core", axis=0)
    half = keep + lax.dynamic_index_in_dim(given, 1 - core, 0, keepdims=False).astype(f32)
    half = half.astype(bf16)
    parts = lax.all_to_all(half, ("x", "y"), split_axis=0, concat_axis=0, tiled=True)
    mixed = (hidden + jnp.sum(parts.astype(f32), axis=0)).astype(bf16)
    back = lax.all_to_all(
        mixed.reshape(n_z, SLOTS, width), "z", split_axis=0, concat_axis=0, tiled=True
    )
    back = back.reshape(slots, width)
    out = jnp.einsum("sr,sc->rc", table, back, preferred_element_type=f32)
    return out.astype(bf16)


def solution(mesh):
    n_x = GROUP
    n_z = mesh.shape["dp"] // n_x
    n_y = mesh.shape["cuts"] // CORES
    fine = Mesh(mesh.devices.reshape(n_z, n_x, n_y, CORES), ("z", "x", "y", "core"))
    rows, cols = ("z", "x"), ("y", "core")
    placed = (
        P(rows, cols),
        P(rows, cols),
        P(rows, cols),
        P(rows, None, cols),
        P(rows, None, cols),
        P(rows),
        P(rows, None),
        P(),
        P(cols, None),
        P(rows, None),
        P(rows, None, cols),
        P(rows, cols, None),
    )
    return jax.shard_map(
        on_device, mesh=fine, in_specs=placed, out_specs=P(rows, cols), check_vma=False
    )
```

time: 90.3 us -> 84.3 us (0.934)
  Pallas kernels: 7.26 us -> 2.69 us
    pallas_call x1, Pallas kernels: 4.05 us -> 0.87 us  [run_expert(): pl.pallas_call(functools.partial(expert_kernel, n_x, n_y), out_shape=(in_...]
    pallas_call x1, Pallas kernels: 3.21 us -> 1.82 us  [attend(): pl.pallas_call(functools.partial(attend_kernel, n_y), out_shape=(half, ha...]
where the time goes in v3:
time: 84.3 us; the launch traced here: 83.5 us
  blocking collectives  79.4 us (94%)
  Pallas kernels  2.69 us (3%)
  matrix products  0.92 us (1%)
    all_to_all x1, blocking collectives, on_device(): lax.all_to_all(packed, ('z', 'y'), split_axis=0, concat_axis=0, tiled=True)  27 us
    all_to_all x1, blocking collectives, on_device(): lax.all_to_all(mixed.reshape(n_z, SLOTS, width), 'z', split_axis=0, conca...  13.8 us
    all_to_all x1, blocking collectives, on_device(): lax.all_to_all(spread, ('x', 'y'), split_axis=0, concat_axis=0, tiled=True)  12 us
    all_to_all x1, blocking collectives, on_device(): lax.all_to_all(half, ('x', 'y'), split_axis=0, concat_axis=0, tiled=True)  10.7 us
    all_gather x2, blocking collectives, on_device(): given = lax.all_gather(give, 'core', axis=0)  10.6 us
    all_gather x1, blocking collectives, on_device(): pair = lax.all_gather(plane, 'core', axis=0)  5.17 us
    pallas_call x1, Pallas kernels, attend(): pl.pallas_call(functools.partial(attend_kernel, n_y), out_shape=(half, ha...  1.82 us

profile of v3, /device:TPU:1, one launch (start us, length us, event | category | flops | bytes accessed | tf_op | source)
XLA Modules:
  0.0 83.5 jit_solution(6305299052056323960)
XLA Ops:
  0.0 1.8 %attend.1 = (f32[8,1024]{1,0:T(8,128)S(1)}, f32[8,1024]{1,0:T(8,128)S(1)}, bf16[32,8]{1,0:T(8,128)(2,1)S(1)}) custom-call(s32[8]{0:T(128)} %refs_0_.1, s32[8]{0:T(128)} %bitcast.41, bf16[8,256]{1,0:T(8,128)(2,1)} %refs_2_.1, bf16[512,256]{1,0:T(8,128)(2,1)} %bitcast.37, bf16[8,256]{1,0:T(8,128)(2,1)} %refs_4_.1, bf16[512,256]{1,0:T(8,128)(2,1)} %bitcast.38, ...), custom_call_target="tpu_custom_call" | custom-call | tf_op jit(solution)/shard_map/attend/pallas_call | solution.py:123
  1.8 8.4 %all-gather = f32[16,1024]{1,0:T(8,128)S(1)} all-gather(f32[8,1024]{1,0:T(8,128)S(1)} %get-tuple-element.12), channel_id=2, replica_groups=mesh['z'=16,'x'=4,'y'=4,'core'=2] {'core'}, dimensions={0}, use_global_device_ids=true | all-gather | bytes 98304 | tf_op jit(solution)/shard_map/all_gather | solution.py:218
  10.2 0.1 convolution_convert_fusion
  10.4 0.0 copy-start.1
  10.4 0.0 copy-start
  10.5 27.0 %all_to_all.20 = bf16[64,2,256]{2,1,0:T(2,128)(2,1)S(1)} all-to-all(bf16[64,2,256]{2,1,0:T(2,128)(2,1)S(1)} %bitcast.36), channel_id=1, replica_groups=mesh['z'=16,'x'=4,'y'=4,'core'=2] {'z','y'}, dimensions={0} | all-to-all | bytes 131072 | tf_op jit(solution)/shard_map/all_to_all | solution.py:224
  37.5 0.1 convert_reduce_fusion.1
  37.6 12.0 %all_to_all.21 = bf16[16,32,256]{2,1,0:T(8,128)(2,1)S(1)} all-to-all(bf16[16,32,256]{2,1,0:T(8,128)(2,1)S(1)} %broadcast_in_dim.4), channel_id=1, replica_groups=mesh['z'=16,'x'=4,'y'=4,'core'=2] {'x','y'}, dimensions={0} | all-to-all | bytes 524288 | tf_op jit(solution)/shard_map/all_to_all | solution.py:228
  49.7 0.0 copy-start.2
  49.7 5.2 %all-gather.1 = bf16[32,32,256]{2,1,0:T(8,128)(2,1)S(1)} all-gather(bf16[16,32,256]{2,1,0:T(8,128)(2,1)S(1)} %all_to_all.21), channel_id=3, replica_groups=mesh['z'=16,'x'=4,'y'=4,'core'=2] {'core'}, dimensions={0}, use_global_device_ids=true | all-gather | bytes 786432 | tf_op jit(solution)/shard_map/all_gather | solution.py:229
  54.8 0.0 copy-done.1
  54.8 0.0 copy-done
  54.8 0.0 copy-done.2
  54.8 0.9 %expert.1 = (f32[16,32,256]{2,1,0:T(8,128)S(1)}, bf16[16,32,256]{2,1,0:T(8,128)(2,1)S(1)}) custom-call(bf16[2,16,32,256]{3,2,1,0:T(8,128)(2,1)S(1)} %bitcast.31, f32[1,2048]{1,0:T(1,128)S(1)} %bitcast.34, bf16[2048,256]{1,0:T(8,128)(2,1)S(1)} %bitcast.32, bf16[256,2048]{1,0:T(8,128)(2,1)S(1)} %bitcast.33), custom_call_target="tpu_custom_call" | custom-call | tf_op jit(solution)/shard_map/expert/pallas_call | solution.py:171
  55.7 2.2 %all-gather.2 = bf16[32,32,256]{2,1,0:T(8,128)(2,1)S(1)} all-gather(bf16[16,32,256]{2,1,0:T(8,128)(2,1)S(1)} %get-tuple-element.14), channel_id=4, replica_groups=mesh['z'=16,'x'=4,'y'=4,'core'=2] {'core'}, dimensions={0}, use_global_device_ids=true | all-gather | bytes 786432 | tf_op jit(solution)/shard_map/all_gather | solution.py:231
  57.9 0.1 fusion
  58.0 10.7 %all_to_all.22 = bf16[16,32,256]{2,1,0:T(8,128)(2,1)S(1)} all-to-all(bf16[16,32,256]{2,1,0:T(8,128)(2,1)S(1)} %fusion), channel_id=1, replica_groups=mesh['z'=16,'x'=4,'y'=4,'core'=2] {'x','y'}, dimensions={0} | all-to-all | bytes 524288 | tf_op jit(solution)/shard_map/all_to_all | solution.py:234
  68.9 13.8 %all_to_all.23 = bf16[16,2,256]{2,1,0:T(2,128)(2,1)S(1)} all-to-all(bf16[16,2,256]{2,1,0:T(2,128)(2,1)S(1)} %add_convert_fusion), channel_id=1, replica_groups=mesh['z'=16,'x'=4,'y'=4,'core'=2] {'z'}, dimensions={0} | all-to-all | bytes 32768 | tf_op jit(solution)/shard_map/all_to_all | solution.py:236
  82.7 0.8 convolution_convert_fusion.1
  (10 shorter events, 0.2 us)
Async XLA Ops:
  10.4 44.5 %copy-start.1 = (bf16[1,256,2048]{2,1,0:T(8,128)(2,1)S(1)}, bf16[1,256,2048]{2,1,0:T(8,128)(2,1)}, u32[]{:S(2)}) copy-start(bf16[1,256,2048]{2,1,0:T(8,128)(2,1)} %param.23) | copy-start | bytes 3145732
  10.4 44.4 %copy-start = (bf16[1,2048,256]{2,1,0:T(8,128)(2,1)S(1)}, bf16[1,2048,256]{2,1,0:T(8,128)(2,1)}, u32[]{:S(2)}) copy-start(bf16[1,2048,256]{2,1,0:T(8,128)(2,1)} %param.22) | copy-start | bytes 3145732
  49.7 5.2 %copy-start.2 = (f32[2048]{0:T(1024)S(1)}, f32[2048]{0:T(1024)}, u32[]{:S(2)}) copy-start(f32[2048]{0:T(1024)} %param.19) | copy-start | bytes 24580

commit v4 on v3

--- a/solution.py
+++ b/solution.py
@@ -131,9 +131,8 @@
     )(*args)
 
 
-def expert_kernel(n_x, n_y, pair, gain, up, down, keep, give, normed):
+def expert_kernel(n_x, n_y, pair, gain, up, down, pieces, normed):
     f32, bf16 = jnp.float32, jnp.bfloat16
-    core = lax.axis_index("core")
     slots, width = pair.shape[2:]
     width_all = n_y * CORES * width
     blocks = [(y, c) for y in range(n_y) for c in range(CORES)]
@@ -151,15 +150,10 @@
     units = jnp.dot(normed[...], up[...], preferred_element_type=f32)
     act = jax.nn.gelu(units).astype(bf16)
     for y in range(n_y):
-        both = []
-        for c in range(CORES):
-            cols = pl.ds((y * CORES + c) * width, width)
-            both.append(jnp.dot(act, down[:, cols], preferred_element_type=f32))
-        own = jnp.where(core == 0, both[0], both[1])
-        other = jnp.where(core == 0, both[1], both[0]).astype(bf16)
+        cols = pl.ds(y * CORES * width, CORES * width)
+        piece = jnp.dot(act, down[:, cols], preferred_element_type=f32).astype(bf16)
         for x in range(n_x):
-            keep[x * n_y + y] = own[x * slots : (x + 1) * slots]
-            give[x * n_y + y] = other[x * slots : (x + 1) * slots]
+            pieces[x * n_y + y] = piece[x * slots : (x + 1) * slots]
 
 
 def run_expert(n_x, n_y, pair, norm_gain, w_up, w_down):
@@ -170,12 +164,9 @@
     ]
     return pl.pallas_call(
         functools.partial(expert_kernel, n_x, n_y),
-        out_shape=(
-            in_vmem(pair.shape[1:], jnp.float32),
-            in_vmem(pair.shape[1:], jnp.bfloat16),
-        ),
+        out_shape=in_vmem(pair.shape[1:3] + (CORES * pair.shape[3],), jnp.bfloat16),
         in_specs=[vmem] * 4,
-        out_specs=(vmem, vmem),
+        out_specs=vmem,
         scratch_shapes=[pltpu.VMEM((n_x * pair.shape[2], w_up.shape[0]), jnp.bfloat16)],
         name="expert",
     )(*args)
@@ -227,17 +218,16 @@
     spread = jnp.broadcast_to(hidden.astype(bf16)[None], (n_x * n_y, slots, width))
     plane = lax.all_to_all(spread, ("x", "y"), split_axis=0, concat_axis=0, tiled=True)
     pair = lax.all_gather(plane, "core", axis=0)
-    keep, give = run_expert(n_x, n_y, pair, norm_gain, w_up[0], w_down[0])
-    given = lax.all_gather(give, "core", axis=0)
-    half = keep + lax.dynamic_index_in_dim(given, 1 - core, 0, keepdims=False).astype(f32)
-    half = half.astype(bf16)
-    parts = lax.all_to_all(half, ("x", "y"), split_axis=0, concat_axis=0, tiled=True)
-    mixed = (hidden + jnp.sum(parts.astype(f32), axis=0)).astype(bf16)
-    back = lax.all_to_all(
-        mixed.reshape(n_z, SLOTS, width), "z", split_axis=0, concat_axis=0, tiled=True
-    )
-    back = back.reshape(slots, width)
-    out = jnp.einsum("sr,sc->rc", table, back, preferred_element_type=f32)
+    pieces = run_expert(n_x, n_y, pair, norm_gain, w_up[0], w_down[0])
+    parts = lax.all_to_all(pieces, ("x", "y"), split_axis=0, concat_axis=0, tiled=True)
+    both = jnp.sum(parts.astype(f32), axis=0).reshape(n_z, SLOTS, CORES, width)
+    mine = (jnp.arange(CORES) == core)[None, None, :, None]
+    both = both + jnp.where(mine, hidden.reshape(n_z, SLOTS, 1, width), 0.0)
+    both = both.astype(bf16).transpose(0, 2, 1, 3).reshape(n_z * CORES, SLOTS, width)
+    back = lax.all_to_all(both, ("z", "core"), split_axis=0, concat_axis=0, tiled=True)
+    back = back.reshape(n_z, CORES, SLOTS, width)
+    spots = table.reshape(n_z, SLOTS, count)
+    out = jnp.einsum("zsr,zksc->rc", spots, back, preferred_element_type=f32)
     return out.astype(bf16)
 
 

time: 84.3 us -> 88.9 us (1.055)
  waiting for transfers between devices: 0 us -> 10.4 us
  blocking collectives: 79.4 us -> 69.5 us
  starting transfers between devices: 0 us -> 3.57 us
    all_to_all x0 -> x1, waiting for transfers between devices: none -> 10.4 us  [on_device(): lax.all_to_all(pieces, ('x', 'y'), split_axis=0, concat_axis=0, tiled=True)]
    all_to_all x2 -> x1, blocking collectives: 24.6 us -> 16.9 us  [on_device(): lax.all_to_all(both, ('z', 'core'), split_axis=0, concat_axis=0, tiled=True)]
    all_to_all x0 -> x1, starting transfers between devices: none -> 3.57 us  [on_device(): lax.all_to_all(pieces, ('x', 'y'), split_axis=0, concat_axis=0, tiled=True)]
    all_gather x2 -> x1, blocking collectives: 10.6 us -> 8.38 us  [on_device(): given = lax.all_gather(give, 'core', axis=0)]
  transfers between devices with their start and end apart: 0 -> 1, of which waited for: 0 -> 1; matrix products, arithmetic and copies ran while one was open for 0% -> 0% of each run, Pallas kernels for 0% -> 0%
where the time goes in v4:
time: 88.9 us; the launch traced here: 88.5 us
  blocking collectives  69.5 us (78%)
  waiting for transfers between devices  10.4 us (12%)
  starting transfers between devices  3.57 us (4%)
  Pallas kernels  3.48 us (4%)
  matrix products  0.92 us (1%)
    all_to_all x1, blocking collectives, on_device(): lax.all_to_all(packed, ('z', 'y'), split_axis=0, concat_axis=0, tiled=True)  27 us
    all_to_all x1, blocking collectives, on_device(): lax.all_to_all(both, ('z', 'core'), split_axis=0, concat_axis=0, tiled=True)  16.9 us
    all_to_all x1, blocking collectives, on_device(): lax.all_to_all(spread, ('x', 'y'), split_axis=0, concat_axis=0, tiled=True)  12 us
    all_to_all x1, waiting for transfers between devices, on_device(): lax.all_to_all(pieces, ('x', 'y'), split_axis=0, concat_axis=0, tiled=True)  10.4 us
    all_gather x1, blocking collectives, on_device(): given = lax.all_gather(give, 'core', axis=0)  8.38 us
    all_gather x1, blocking collectives, on_device(): pair = lax.all_gather(plane, 'core', axis=0)  5.17 us
    all_to_all x1, starting transfers between devices, on_device(): lax.all_to_all(pieces, ('x', 'y'), split_axis=0, concat_axis=0, tiled=True)  3.57 us
    pallas_call x1, Pallas kernels, attend(): pl.pallas_call(functools.partial(attend_kernel, n_y), out_shape=(half, ha...  1.82 us
  transfers between devices with their start and end apart: 1, of which 1 were waited for; matrix products, arithmetic and copies ran while one was open for 0% of the time, Pallas kernels for 0%

profile of v4, /device:TPU:1, one launch (start us, length us, event | category | flops | bytes accessed | tf_op | source)
XLA Modules:
  0.0 88.5 jit_solution(11174932418473527698)
XLA Ops:
  0.0 1.8 %attend.1 = (f32[8,1024]{1,0:T(8,128)S(1)}, f32[8,1024]{1,0:T(8,128)S(1)}, bf16[32,8]{1,0:T(8,128)(2,1)S(1)}) custom-call(s32[8]{0:T(128)} %refs_0_.1, s32[8]{0:T(128)} %bitcast.47, bf16[8,256]{1,0:T(8,128)(2,1)} %refs_2_.1, bf16[512,256]{1,0:T(8,128)(2,1)} %bitcast.42, bf16[8,256]{1,0:T(8,128)(2,1)} %refs_4_.1, bf16[512,256]{1,0:T(8,128)(2,1)} %bitcast.43, ...), custom_call_target="tpu_custom_call" | custom-call | tf_op jit(solution)/shard_map/attend/pallas_call | solution.py:123
  1.8 8.4 %all-gather = f32[16,1024]{1,0:T(8,128)S(1)} all-gather(f32[8,1024]{1,0:T(8,128)S(1)} %get-tuple-element.10), channel_id=2, replica_groups=mesh['z'=16,'x'=4,'y'=4,'core'=2] {'core'}, dimensions={0}, use_global_device_ids=true | all-gather | bytes 98304 | tf_op jit(solution)/shard_map/all_gather | solution.py:209
  10.2 0.1 convolution_convert_fusion
  10.4 0.0 copy-start.1
  10.4 0.0 copy-start
  10.5 27.0 %all_to_all.20 = bf16[64,2,256]{2,1,0:T(2,128)(2,1)S(1)} all-to-all(bf16[64,2,256]{2,1,0:T(2,128)(2,1)S(1)} %bitcast.41), channel_id=1, replica_groups=mesh['z'=16,'x'=4,'y'=4,'core'=2] {'z','y'}, dimensions={0} | all-to-all | bytes 131072 | tf_op jit(solution)/shard_map/all_to_all | solution.py:215
  37.5 0.1 convert_reduce_fusion.1
  37.6 12.0 %all_to_all.21 = bf16[16,32,256]{2,1,0:T(8,128)(2,1)S(1)} all-to-all(bf16[16,32,256]{2,1,0:T(8,128)(2,1)S(1)} %broadcast_in_dim.30), channel_id=1, replica_groups=mesh['z'=16,'x'=4,'y'=4,'core'=2] {'x','y'}, dimensions={0} | all-to-all | bytes 524288 | tf_op jit(solution)/shard_map/all_to_all | solution.py:219
  49.7 0.0 copy-start.2
  49.7 5.2 %all-gather.1 = bf16[32,32,256]{2,1,0:T(8,128)(2,1)S(1)} all-gather(bf16[16,32,256]{2,1,0:T(8,128)(2,1)S(1)} %all_to_all.21), channel_id=3, replica_groups=mesh['z'=16,'x'=4,'y'=4,'core'=2] {'core'}, dimensions={0}, use_global_device_ids=true | all-gather | bytes 786432 | tf_op jit(solution)/shard_map/all_gather | solution.py:220
  54.8 0.0 copy-done.1
  54.8 0.0 copy-done
  54.8 0.0 copy-done.2
  54.8 1.7 %expert.1 = bf16[16,32,512]{2,1,0:T(8,128)(2,1)} custom-call(bf16[2,16,32,256]{3,2,1,0:T(8,128)(2,1)S(1)} %bitcast.36, f32[1,2048]{1,0:T(1,128)S(1)} %bitcast.40, bf16[2048,256]{1,0:T(8,128)(2,1)S(1)} %bitcast.37, bf16[256,2048]{1,0:T(8,128)(2,1)S(1)} %bitcast.38), custom_call_target="tpu_custom_call" | custom-call | tf_op jit(solution)/shard_map/expert/pallas_call | solution.py:165
  56.5 3.6 %all-to-all-start.2 = ((bf16[16,32,512]{2,1,0:T(8,128)(2,1)}), bf16[16,32,512]{2,1,0:T(8,128)(2,1)S(1)}, u32[]{:S(2)}, u32[]{:S(2)}) async-start(bf16[16,32,512]{2,1,0:T(8,128)(2,1)} %expert.1), calls=%async_computation.2 | async-start | bytes 1048576 | tf_op jit(solution)/shard_map/all_to_all | solution.py:222
  60.1 10.4 %all-to-all-done.2 = bf16[16,32,512]{2,1,0:T(8,128)(2,1)S(1)} async-done(((bf16[16,32,512]{2,1,0:T(8,128)(2,1)}), bf16[16,32,512]{2,1,0:T(8,128)(2,1)S(1)}, u32[]{:S(2)}, u32[]{:S(2)}) %all-to-all-start.2) | async-done | bytes 524320 | tf_op jit(solution)/shard_map/all_to_all | solution.py:222
  70.5 0.1 convert_reduce_fusion
  70.7 0.1 fusion.3
  70.8 16.9 %all_to_all.22 = bf16[32,2,256]{2,1,0:T(2,128)(2,1)S(1)} all-to-all(bf16[32,2,256]{2,1,0:T(2,128)(2,1)S(1)} %bitcast.45), channel_id=1, replica_groups=mesh['z'=16,'x'=4,'y'=4,'core'=2] {'z','core'}, dimensions={0} | all-to-all | bytes 65536 | tf_op jit(solution)/shard_map/all_to_all | solution.py:227
  87.7 0.8 fusion
  (10 shorter events, 0.2 us)
Async XLA Ops:
  10.4 44.5 %copy-start.1 = (bf16[1,256,2048]{2,1,0:T(8,128)(2,1)S(1)}, bf16[1,256,2048]{2,1,0:T(8,128)(2,1)}, u32[]{:S(2)}) copy-start(bf16[1,256,2048]{2,1,0:T(8,128)(2,1)} %param.23) | copy-start | bytes 3145732
  10.4 44.4 %copy-start = (bf16[1,2048,256]{2,1,0:T(8,128)(2,1)S(1)}, bf16[1,2048,256]{2,1,0:T(8,128)(2,1)}, u32[]{:S(2)}) copy-start(bf16[1,2048,256]{2,1,0:T(8,128)(2,1)} %param.22) | copy-start | bytes 3145732
  49.7 5.2 %copy-start.2 = (f32[2048]{0:T(1024)S(1)}, f32[2048]{0:T(1024)}, u32[]{:S(2)}) copy-start(f32[2048]{0:T(1024)} %param.19) | copy-start | bytes 24580
  56.5 14.0 %all-to-all-start.2 = ((bf16[16,32,512]{2,1,0:T(8,128)(2,1)}), bf16[16,32,512]{2,1,0:T(8,128)(2,1)S(1)}, u32[]{:S(2)}, u32[]{:S(2)}) async-start(bf16[16,32,512]{2,1,0:T(8,128)(2,1)} %expert.1), calls=%async_computation.2 | async-start | bytes 1048576 | tf_op jit(solution)/shard_map/all_to_all | solution.py:222

commit v5 on v3

--- a/solution.py
+++ b/solution.py
@@ -131,54 +131,80 @@
     )(*args)
 
 
-def expert_kernel(n_x, n_y, pair, gain, up, down, keep, give, normed):
+def units_kernel(n_x, n_y, plane, gain, up, up_other, partial):
     f32, bf16 = jnp.float32, jnp.bfloat16
     core = lax.axis_index("core")
-    slots, width = pair.shape[2:]
-    width_all = n_y * CORES * width
-    blocks = [(y, c) for y in range(n_y) for c in range(CORES)]
-    for x in range(n_x):
-        squares = jnp.zeros((slots, width), f32)
-        for y, c in blocks:
-            block = pair[c, x * n_y + y].astype(f32)
-            squares = squares + block * block
-        meansq = jnp.sum(squares, axis=-1, keepdims=True) * (1.0 / width_all)
-        inverse = lax.rsqrt(meansq + 1e-06)
-        for y, c in blocks:
-            cols = pl.ds((y * CORES + c) * width, width)
-            block = pair[c, x * n_y + y].astype(f32) * inverse * gain[:, cols]
-            normed[pl.ds(x * slots, slots), cols] = block.astype(bf16)
-    units = jnp.dot(normed[...], up[...], preferred_element_type=f32)
-    act = jax.nn.gelu(units).astype(bf16)
+    slots, width = plane.shape[1:]
+    units = up.shape[1]
+    rows = n_x * slots
+    own = jnp.zeros((rows, units), f32)
+    other = jnp.zeros((rows, units), f32)
+    squares = jnp.zeros((rows, width), f32)
     for y in range(n_y):
-        both = []
-        for c in range(CORES):
-            cols = pl.ds((y * CORES + c) * width, width)
-            both.append(jnp.dot(act, down[:, cols], preferred_element_type=f32))
-        own = jnp.where(core == 0, both[0], both[1])
-        other = jnp.where(core == 0, both[1], both[0]).astype(bf16)
+        block = [plane[x * n_y + y].astype(f32) for x in range(n_x)]
+        block = jnp.concatenate(block, axis=0)
+        squares = squares + block * block
+        low = gain[:, pl.ds(y * CORES * width, width)]
+        high = gain[:, pl.ds((y * CORES + 1) * width, width)]
+        scaled = (block * jnp.where(core == 0, low, high)).astype(bf16)
+        start = pl.multiple_of((y * CORES + core) * width, width)
+        own = own + jnp.dot(scaled, up[pl.ds(start, width), :], preferred_element_type=f32)
+        other = other + jnp.dot(scaled, up_other[y], preferred_element_type=f32)
+    partial[:, pl.ds(0, units)] = jnp.where(core == 0, own, other)
+    partial[:, pl.ds(units, units)] = jnp.where(core == 0, other, own)
+    total = jnp.sum(squares, axis=-1, keepdims=True)
+    partial[:, pl.ds(CORES * units, HD)] = jnp.broadcast_to(total, (rows, HD))
+
+
+def down_kernel(n_x, n_y, width_all, partials, down, down_other, half):
+    f32, bf16 = jnp.float32, jnp.bfloat16
+    core = lax.axis_index("core")
+    units = down.shape[0]
+    slots, width = half.shape[1:]
+    squares = partials[0, :, pl.ds(CORES * units, HD)] + partials[1, :, pl.ds(CORES * units, HD)]
+    inverse = lax.rsqrt(squares[:, :1] * (1.0 / width_all) + 1e-06)
+    acts = []
+    for c in range(CORES):
+        cols = pl.ds(c * units, units)
+        summed = (partials[0, :, cols] + partials[1, :, cols]) * inverse
+        acts.append(jax.nn.gelu(summed).astype(bf16))
+    own = jnp.where(core == 0, acts[0], acts[1])
+    other = jnp.where(core == 0, acts[1], acts[0])
+    for y in range(n_y):
+        start = pl.multiple_of((y * CORES + core) * width, width)
+        piece = jnp.dot(own, down[:, pl.ds(start, width)], preferred_element_type=f32)
+        cols = pl.ds(y * width, width)
+        piece = piece + jnp.dot(other, down_other[:, cols], preferred_element_type=f32)
+        piece = piece.astype(bf16)
         for x in range(n_x):
-            keep[x * n_y + y] = own[x * slots : (x + 1) * slots]
-            give[x * n_y + y] = other[x * slots : (x + 1) * slots]
-
-
-def run_expert(n_x, n_y, pair, norm_gain, w_up, w_down):
+            half[x * n_y + y] = piece[x * slots : (x + 1) * slots]
+
+
+def held_in_vmem(*args):
+    return [pltpu.with_memory_space_constraint(arg, pltpu.VMEM) for arg in args]
+
+
+def run_units(n_x, n_y, plane, norm_gain, w_up, up_other):
     vmem = pl.BlockSpec(memory_space=pltpu.VMEM)
-    args = [
-        pltpu.with_memory_space_constraint(arg, pltpu.VMEM)
-        for arg in (pair, norm_gain[None, :], w_up, w_down)
-    ]
+    shape = (n_x * plane.shape[1], CORES * w_up.shape[1] + HD)
     return pl.pallas_call(
-        functools.partial(expert_kernel, n_x, n_y),
-        out_shape=(
-            in_vmem(pair.shape[1:], jnp.float32),
-            in_vmem(pair.shape[1:], jnp.bfloat16),
-        ),
+        functools.partial(units_kernel, n_x, n_y),
+        out_shape=in_vmem(shape, jnp.float32),
         in_specs=[vmem] * 4,
-        out_specs=(vmem, vmem),
-        scratch_shapes=[pltpu.VMEM((n_x * pair.shape[2], w_up.shape[0]), jnp.bfloat16)],
-        name="expert",
-    )(*args)
+        out_specs=vmem,
+        name="units",
+    )(*held_in_vmem(plane, norm_gain[None, :], w_up, up_other))
+
+
+def run_down(n_x, n_y, width_all, shape, partials, w_down, down_other):
+    vmem = pl.BlockSpec(memory_space=pltpu.VMEM)
+    return pl.pallas_call(
+        functools.partial(down_kernel, n_x, n_y, width_all),
+        out_shape=in_vmem(shape, jnp.bfloat16),
+        in_specs=[vmem] * 3,
+        out_specs=vmem,
+        name="down",
+    )(*held_in_vmem(partials, w_down, down_other))
 
 
 def on_device(
@@ -221,16 +247,22 @@
     packed = jnp.einsum("sr,ryc->syc", table, chip, preferred_element_type=f32)
     packed = packed.astype(bf16).reshape(n_z, SLOTS, n_y, width).transpose(0, 2, 1, 3)
     packed = packed.reshape(n_z * n_y, SLOTS, width)
+    packed, up, down = lax.optimization_barrier((packed, w_up[0], w_down[0]))
+    swap = [(0, 1), (1, 0)]
+    up_give = up.reshape(n_y, CORES, width, up.shape[1])
+    up_give = lax.dynamic_index_in_dim(up_give, 1 - core, 1, keepdims=False)
+    up_other = lax.ppermute(up_give, "core", swap)
+    down_give = down.reshape(down.shape[0], n_y, CORES, width)
+    down_give = lax.dynamic_index_in_dim(down_give, 1 - core, 2, keepdims=False)
+    down_other = lax.ppermute(down_give.reshape(down.shape[0], n_y * width), "core", swap)
     got = lax.all_to_all(packed, ("z", "y"), split_axis=0, concat_axis=0, tiled=True)
     hidden = jnp.sum(got.reshape(n_z, n_y, SLOTS, width).astype(f32), axis=1).reshape(slots, width)
 
     spread = jnp.broadcast_to(hidden.astype(bf16)[None], (n_x * n_y, slots, width))
     plane = lax.all_to_all(spread, ("x", "y"), split_axis=0, concat_axis=0, tiled=True)
-    pair = lax.all_gather(plane, "core", axis=0)
-    keep, give = run_expert(n_x, n_y, pair, norm_gain, w_up[0], w_down[0])
-    given = lax.all_gather(give, "core", axis=0)
-    half = keep + lax.dynamic_index_in_dim(given, 1 - core, 0, keepdims=False).astype(f32)
-    half = half.astype(bf16)
+    partial = run_units(n_x, n_y, plane, norm_gain, up, up_other)
+    partials = lax.all_gather(partial, "core", axis=0)
+    half = run_down(n_x, n_y, width_all, plane.shape, partials, down, down_other)
     parts = lax.all_to_all(half, ("x", "y"), split_axis=0, concat_axis=0, tiled=True)
     mixed = (hidden + jnp.sum(parts.astype(f32), axis=0)).astype(bf16)
     back = lax.all_to_all(

time: 84.3 us -> 91.1 us (1.081)
  blocking collectives: 79.4 us -> 55.9 us
  starting transfers between devices: 0 us -> 17.5 us
  local copies, waits for them, and re-layouts: 0.16 us -> 7.89 us
  waiting for transfers between devices: 0 us -> 3.73 us
  Pallas kernels: 2.69 us -> 3.69 us
    all_to_all x1 -> x0, blocking collectives: 27 us -> none  [on_device(): lax.all_to_all(packed, ('z', 'y'), split_axis=0, concat_axis=0, tiled=True)]
    all_to_all x0 -> x1, starting transfers between devices: none -> 13.1 us  [on_device(): lax.all_to_all(packed, ('z', 'y'), split_axis=0, concat_axis=0, tiled=True)]
    all_to_all x1, blocking collectives: 13.8 us -> 19.2 us  [on_device(): lax.all_to_all(mixed.reshape(n_z, SLOTS, width), 'z', split_axis=0, conca...]
    ppermute x0 -> x2, starting transfers between devices: none -> 4.43 us  [the longest x1 2.52 us: on_device(): up_other = lax.ppermute(up_give, 'core', swap)]
    all_to_all x0 -> x1, waiting for transfers between devices: none -> 3.72 us  [on_device(): lax.all_to_all(packed, ('z', 'y'), split_axis=0, concat_axis=0, tiled=True)]
    dynamic_slice x0 -> x1, local copies, waits for them, and re-layouts: none -> 3.27 us  [on_device(): down_give = lax.dynamic_index_in_dim(down_give, 1 - core, 2, keepdims=False)]
    unnamed x6 -> x13, local copies, waits for them, and re-layouts: 0.01 us -> 2.21 us
    all_gather x2 -> x1, blocking collectives: 10.6 us -> 8.52 us  [on_device(): given = lax.all_gather(give, 'core', axis=0)]
  transfers between devices with their start and end apart: 0 -> 3, of which waited for: 0 -> 1; matrix products, arithmetic and copies ran while one was open for 0% -> 7% of each run, Pallas kernels for 0% -> 0%
where the time goes in v5:
time: 91.1 us; the launch traced here: 89.9 us
  blocking collectives  55.9 us (61%)
  starting transfers between devices  17.5 us (19%)
  local copies, waits for them, and re-layouts  7.89 us (9%)
  waiting for transfers between devices  3.73 us (4%)
  Pallas kernels  3.69 us (4%)
  matrix products  0.92 us (1%)
    all_to_all x1, blocking collectives, on_device(): lax.all_to_all(mixed.reshape(n_z, SLOTS, width), 'z', split_axis=0, conca...  19.2 us
    all_to_all x1, starting transfers between devices, on_device(): lax.all_to_all(packed, ('z', 'y'), split_axis=0, concat_axis=0, tiled=True)  13.1 us
    all_to_all x1, blocking collectives, on_device(): lax.all_to_all(spread, ('x', 'y'), split_axis=0, concat_axis=0, tiled=True)  12.1 us
    all_to_all x1, blocking collectives, on_device(): lax.all_to_all(half, ('x', 'y'), split_axis=0, concat_axis=0, tiled=True)  10.7 us
    all_gather x1, blocking collectives, on_device(): given = lax.all_gather(give, 'core', axis=0)  8.52 us
    all_gather x1, blocking collectives, on_device(): partials = lax.all_gather(partial, 'core', axis=0)  5.33 us
    all_to_all x1, waiting for transfers between devices, on_device(): lax.all_to_all(packed, ('z', 'y'), split_axis=0, concat_axis=0, tiled=True)  3.72 us
    dynamic_slice x1, local copies, waits for them, and re-layouts, on_device(): down_give = lax.dynamic_index_in_dim(down_give, 1 - core, 2, keepdims=False)  3.27 us
  transfers between devices with their start and end apart: 3, of which 1 were waited for; matrix products, arithmetic and copies ran while one was open for 7% of the time, Pallas kernels for 0%

profile of v5, /device:TPU:1, one launch (start us, length us, event | category | flops | bytes accessed | tf_op | source)
XLA Modules:
  0.0 89.9 jit_solution(12286029556565821490)
XLA Ops:
  0.0 0.0 copy-start.1
  0.0 1.9 %attend.1 = (f32[8,1024]{1,0:T(8,128)S(1)}, f32[8,1024]{1,0:T(8,128)S(1)}, bf16[32,8]{1,0:T(8,128)(2,1)S(1)}) custom-call(s32[8]{0:T(128)} %refs_0_.1, s32[8]{0:T(128)} %bitcast.45, bf16[8,256]{1,0:T(8,128)(2,1)} %refs_2_.1, bf16[512,256]{1,0:T(8,128)(2,1)} %bitcast.41, bf16[8,256]{1,0:T(8,128)(2,1)} %refs_4_.1, bf16[512,256]{1,0:T(8,128)(2,1)} %bitcast.42, ...), custom_call_target="tpu_custom_call" | custom-call | tf_op jit(solution)/shard_map/attend/pallas_call | solution.py:123
  1.9 0.0 copy-start
  1.9 8.5 %all-gather = f32[16,1024]{1,0:T(8,128)S(1)} all-gather(f32[8,1024]{1,0:T(8,128)S(1)} %get-tuple-element.13), channel_id=2, replica_groups=mesh['z'=16,'x'=4,'y'=4,'core'=2] {'core'}, dimensions={0}, use_global_device_ids=true | all-gather | bytes 98304 | tf_op jit(solution)/shard_map/all_gather | solution.py:244
  10.5 0.1 convolution_convert_fusion
  10.6 0.7 copy.17
  11.3 13.1 %all-to-all-start = ((bf16[64,2,256]{2,1,0:T(2,128)(2,1)}), bf16[64,2,256]{2,1,0:T(2,128)(2,1)S(1)}, u32[]{:S(2)}, u32[]{:S(2)}) async-start(bf16[64,2,256]{2,1,0:T(2,128)(2,1)} %bitcast.8), calls=%async_computation | async-start | bytes 131072 | tf_op jit(solution)/shard_map/all_to_all | solution.py:258
  24.4 0.0 copy-done.1
  24.4 0.8 dynamic-slice_bitcast_fusion
  25.2 2.5 %collective-permute-start = (bf16[4,256,256]{2,1,0:T(8,128)(2,1)}, bf16[4,256,256]{2,1,0:T(8,128)(2,1)S(1)}, u32[]{:S(2)}, u32[]{:S(2)}) collective-permute-start(bf16[4,256,256]{2,1,0:T(8,128)(2,1)} %dynamic-slice_bitcast_fusion), channel_id=1, source_target_pairs={{0,1},{1,0},{2,3},{3,2},{4,5},{5,4},{6,7},{7,6},{8,9},{9,8},{10,11... | collective-permute-start | bytes 1572872 | tf_op jit(solution)/shard_map/ppermute | solution.py:254
  27.8 0.0 copy-done
  27.8 0.8 reshape.46
  28.6 3.3 %dynamic-slice_reduce_fusion = bf16[256,4,256]{2,1,0:T(4,128)(2,1)S(1)} fusion(bf16[256,4,2,256]{3,2,1,0:T(2,128)(2,1)S(1)} %reshape.46, s32[]{:T(128)S(6)} %select_n.8), kind=kLoop, calls=%fused_computation.2 | loop fusion | bytes 1048580 | tf_op jit(solution)/shard_map/jit(dynamic_index_in_dim)/dynamic_slice | solution.py:256
  31.9 0.0 copy-start.2
  31.9 0.9 copy.24
  32.8 1.9 %collective-permute-start.1 = (bf16[256,1024]{1,0:T(8,128)(2,1)}, bf16[256,1024]{1,0:T(8,128)(2,1)}, u32[]{:S(2)}, u32[]{:S(2)}) collective-permute-start(bf16[256,1024]{1,0:T(8,128)(2,1)} %bitcast.22), channel_id=1, source_target_pairs={{0,1},{1,0},{2,3},{3,2},{4,5},{5,4},{6,7},{7,6},{8,9},{9,8},{10,11... | collective-permute-start | bytes 1572872 | tf_op jit(solution)/shard_map/ppermute | solution.py:257
  34.7 3.7 %all-to-all-done = bf16[64,2,256]{2,1,0:T(2,128)(2,1)S(1)} async-done(((bf16[64,2,256]{2,1,0:T(2,128)(2,1)}), bf16[64,2,256]{2,1,0:T(2,128)(2,1)S(1)}, u32[]{:S(2)}, u32[]{:S(2)}) %all-to-all-start) | async-done | bytes 65568 | tf_op jit(solution)/shard_map/all_to_all | solution.py:258
  38.4 0.1 convert_reduce_fusion.1
  38.5 0.0 copy-start.4
  38.5 0.6 copy-done.4
  39.1 0.0 copy-start.3
  39.1 12.1 %all_to_all.20.plane = bf16[16,32,256]{2,1,0:T(8,128)(2,1)S(1)} all-to-all(bf16[16,32,256]{2,1,0:T(8,128)(2,1)S(1)} %broadcast_in_dim.4), channel_id=1, replica_groups=mesh['z'=16,'x'=4,'y'=4,'core'=2] {'x','y'}, dimensions={0} | all-to-all | bytes 524288 | tf_op jit(solution)/shard_map/all_to_all | solution.py:262
  51.2 0.0 collective-permute-done.up_other
  51.2 0.0 copy-done.2
  51.2 0.0 copy-done.3
  51.2 0.3 units.1
  51.6 5.3 %all-gather.1 = f32[256,640]{1,0:T(8,128)S(1)} all-gather(f32[128,640]{1,0:T(8,128)S(1)} %units.1), channel_id=3, replica_groups=mesh['z'=16,'x'=4,'y'=4,'core'=2] {'core'}, dimensions={0}, use_global_device_ids=true | all-gather | bytes 983040 | tf_op jit(solution)/shard_map/all_gather | solution.py:264
  56.9 0.0 collective-permute-done.1.down_other
  56.9 1.5 %down.1 = bf16[16,32,256]{2,1,0:T(8,128)(2,1)S(1)} custom-call(f32[2,128,640]{2,1,0:T(8,128)S(1)} %bitcast.36, bf16[256,2048]{1,0:T(8,128)(2,1)S(1)} %bitcast.35, bf16[256,1024]{1,0:T(8,128)(2,1)} %collective-permute-done.1.down_other), custom_call_target="tpu_custom_call" | custom-call | tf_op jit(solution)/shard_map/down/pallas_call | solution.py:201
  58.4 10.7 %all_to_all.21 = bf16[16,32,256]{2,1,0:T(8,128)(2,1)S(1)} all-to-all(bf16[16,32,256]{2,1,0:T(8,128)(2,1)S(1)} %down.1), channel_id=1, replica_groups=mesh['z'=16,'x'=4,'y'=4,'core'=2] {'x','y'}, dimensions={0} | all-to-all | bytes 524288 | tf_op jit(solution)/shard_map/all_to_all | solution.py:266
  69.2 0.0 copy-start.5
  69.2 0.7 copy-done.5
  70.0 19.2 %all_to_all.22 = bf16[16,2,256]{2,1,0:T(2,128)(2,1)S(1)} all-to-all(bf16[16,2,256]{2,1,0:T(2,128)(2,1)S(1)} %add_convert_fusion), channel_id=1, replica_groups=mesh['z'=16,'x'=4,'y'=4,'core'=2] {'z'}, dimensions={0} | all-to-all | bytes 32768 | tf_op jit(solution)/shard_map/all_to_all | solution.py:268
  89.1 0.8 convolution_convert_fusion.1
  (9 shorter events, 0.2 us)
Async XLA Ops:
  0.0 24.4 %copy-start.1 = (bf16[1,2048,256]{2,1,0:T(8,128)(2,1)S(1)}, bf16[1,2048,256]{2,1,0:T(8,128)(2,1)}, u32[]{:S(2)}) copy-start(bf16[1,2048,256]{2,1,0:T(8,128)(2,1)} %param.22) | copy-start | bytes 3145732
  1.9 25.9 %copy-start = (bf16[1,256,2048]{2,1,0:T(8,128)(2,1)S(1)}, bf16[1,256,2048]{2,1,0:T(8,128)(2,1)}, u32[]{:S(2)}) copy-start(bf16[1,256,2048]{2,1,0:T(8,128)(2,1)} %param.23) | copy-start | bytes 3145732
  11.3 27.1 %all-to-all-start = ((bf16[64,2,256]{2,1,0:T(2,128)(2,1)}), bf16[64,2,256]{2,1,0:T(2,128)(2,1)S(1)}, u32[]{:S(2)}, u32[]{:S(2)}) async-start(bf16[64,2,256]{2,1,0:T(2,128)(2,1)} %bitcast.8), calls=%async_computation | async-start | bytes 131072 | tf_op jit(solution)/shard_map/all_to_all | solution.py:258
  25.2 26.0 %collective-permute-start = (bf16[4,256,256]{2,1,0:T(8,128)(2,1)}, bf16[4,256,256]{2,1,0:T(8,128)(2,1)S(1)}, u32[]{:S(2)}, u32[]{:S(2)}) collective-permute-start(bf16[4,256,256]{2,1,0:T(8,128)(2,1)} %dynamic-slice_bitcast_fusion), channel_id=1, source_target_pairs={{0,1},{1,0},{2,3},{3,2},{4,5},{5,4},{6,7},{7,6},{8,9},{9,8},{10,11... | collective-permute-start | bytes 1572872 | tf_op jit(solution)/shard_map/ppermute | solution.py:254
  31.9 19.4 %copy-start.2 = (bf16[1,2048,256]{2,1,0:T(8,128)(2,1)S(1)}, bf16[1,2048,256]{2,1,0:T(8,128)(2,1)}, u32[]{:S(2)}) copy-start(bf16[1,2048,256]{2,1,0:T(8,128)(2,1)} %param.22) | copy-start | bytes 3145732
  32.8 24.1 %collective-permute-start.1 = (bf16[256,1024]{1,0:T(8,128)(2,1)}, bf16[256,1024]{1,0:T(8,128)(2,1)}, u32[]{:S(2)}, u32[]{:S(2)}) collective-permute-start(bf16[256,1024]{1,0:T(8,128)(2,1)} %bitcast.22), channel_id=1, source_target_pairs={{0,1},{1,0},{2,3},{3,2},{4,5},{5,4},{6,7},{7,6},{8,9},{9,8},{10,11... | collective-permute-start | bytes 1572872 | tf_op jit(solution)/shard_map/ppermute | solution.py:257
  38.5 0.6 copy-start.4
  39.1 12.1 %copy-start.3 = (f32[2048]{0:T(1024)S(1)}, f32[2048]{0:T(1024)}, u32[]{:S(2)}) copy-start(f32[2048]{0:T(1024)} %param.19) | copy-start | bytes 24580
  69.2 0.8 copy-start.5

commit v6 on v3

--- a/solution.py
+++ b/solution.py
@@ -131,24 +131,24 @@
     )(*args)
 
 
-def expert_kernel(n_x, n_y, pair, gain, up, down, keep, give, normed):
+def expert_kernel(n_x, n_y, pair, gain, up, down, keep, give):
     f32, bf16 = jnp.float32, jnp.bfloat16
     core = lax.axis_index("core")
     slots, width = pair.shape[2:]
     width_all = n_y * CORES * width
-    blocks = [(y, c) for y in range(n_y) for c in range(CORES)]
-    for x in range(n_x):
-        squares = jnp.zeros((slots, width), f32)
-        for y, c in blocks:
-            block = pair[c, x * n_y + y].astype(f32)
+    rows = n_x * slots
+    squares = jnp.zeros((rows, width), f32)
+    units = jnp.zeros((rows, up.shape[1]), f32)
+    for y in range(n_y):
+        for c in range(CORES):
+            cols = pl.ds((y * CORES + c) * width, width)
+            block = [pair[c, x * n_y + y] for x in range(n_x)]
+            block = jnp.concatenate(block, axis=0).astype(f32)
             squares = squares + block * block
-        meansq = jnp.sum(squares, axis=-1, keepdims=True) * (1.0 / width_all)
-        inverse = lax.rsqrt(meansq + 1e-06)
-        for y, c in blocks:
-            cols = pl.ds((y * CORES + c) * width, width)
-            block = pair[c, x * n_y + y].astype(f32) * inverse * gain[:, cols]
-            normed[pl.ds(x * slots, slots), cols] = block.astype(bf16)
-    units = jnp.dot(normed[...], up[...], preferred_element_type=f32)
+            scaled = (block * gain[:, cols]).astype(bf16)
+            units = units + jnp.dot(scaled, up[cols, :], preferred_element_type=f32)
+    meansq = jnp.sum(squares, axis=-1, keepdims=True) * (1.0 / width_all)
+    units = units * lax.rsqrt(meansq + 1e-06)
     act = jax.nn.gelu(units).astype(bf16)
     for y in range(n_y):
         both = []
@@ -176,7 +176,6 @@
         ),
         in_specs=[vmem] * 4,
         out_specs=(vmem, vmem),
-        scratch_shapes=[pltpu.VMEM((n_x * pair.shape[2], w_up.shape[0]), jnp.bfloat16)],
         name="expert",
     )(*args)
 

time: 84.3 us -> 84.2 us (level)
  no operation moved by 1% of the time
where the time goes in v6:
time: 84.2 us; the launch traced here: 83.4 us
  blocking collectives  79.4 us (94%)
  Pallas kernels  2.64 us (3%)
  matrix products  0.92 us (1%)
    all_to_all x1, blocking collectives, on_device(): lax.all_to_all(packed, ('z', 'y'), split_axis=0, concat_axis=0, tiled=True)  27 us
    all_to_all x1, blocking collectives, on_device(): lax.all_to_all(mixed.reshape(n_z, SLOTS, width), 'z', split_axis=0, conca...  13.8 us
    all_to_all x1, blocking collectives, on_device(): lax.all_to_all(spread, ('x', 'y'), split_axis=0, concat_axis=0, tiled=True)  12 us
    all_to_all x1, blocking collectives, on_device(): lax.all_to_all(half, ('x', 'y'), split_axis=0, concat_axis=0, tiled=True)  10.7 us
    all_gather x2, blocking collectives, on_device(): given = lax.all_gather(give, 'core', axis=0)  10.6 us
    all_gather x1, blocking collectives, on_device(): pair = lax.all_gather(plane, 'core', axis=0)  5.17 us
    pallas_call x1, Pallas kernels, attend(): pl.pallas_call(functools.partial(attend_kernel, n_y), out_shape=(half, ha...  1.82 us

profile of v6, /device:TPU:1, one launch (start us, length us, event | category | flops | bytes accessed | tf_op | source)
XLA Modules:
  0.0 83.4 jit_solution(10173483731333897450)
XLA Ops:
  0.0 1.8 %attend.1 = (f32[8,1024]{1,0:T(8,128)S(1)}, f32[8,1024]{1,0:T(8,128)S(1)}, bf16[32,8]{1,0:T(8,128)(2,1)S(1)}) custom-call(s32[8]{0:T(128)} %refs_0_.1, s32[8]{0:T(128)} %bitcast.41, bf16[8,256]{1,0:T(8,128)(2,1)} %refs_2_.1, bf16[512,256]{1,0:T(8,128)(2,1)} %bitcast.37, bf16[8,256]{1,0:T(8,128)(2,1)} %refs_4_.1, bf16[512,256]{1,0:T(8,128)(2,1)} %bitcast.38, ...), custom_call_target="tpu_custom_call" | custom-call | tf_op jit(solution)/shard_map/attend/pallas_call | solution.py:123
  1.8 8.4 %all-gather = f32[16,1024]{1,0:T(8,128)S(1)} all-gather(f32[8,1024]{1,0:T(8,128)S(1)} %get-tuple-element.12), channel_id=2, replica_groups=mesh['z'=16,'x'=4,'y'=4,'core'=2] {'core'}, dimensions={0}, use_global_device_ids=true | all-gather | bytes 98304 | tf_op jit(solution)/shard_map/all_gather | solution.py:217
  10.2 0.1 convolution_convert_fusion
  10.4 0.0 copy-start.1
  10.4 0.0 copy-start
  10.5 27.0 %all_to_all.20 = bf16[64,2,256]{2,1,0:T(2,128)(2,1)S(1)} all-to-all(bf16[64,2,256]{2,1,0:T(2,128)(2,1)S(1)} %bitcast.36), channel_id=1, replica_groups=mesh['z'=16,'x'=4,'y'=4,'core'=2] {'z','y'}, dimensions={0} | all-to-all | bytes 131072 | tf_op jit(solution)/shard_map/all_to_all | solution.py:223
  37.5 0.1 convert_reduce_fusion.1
  37.6 12.0 %all_to_all.21 = bf16[16,32,256]{2,1,0:T(8,128)(2,1)S(1)} all-to-all(bf16[16,32,256]{2,1,0:T(8,128)(2,1)S(1)} %broadcast_in_dim.4), channel_id=1, replica_groups=mesh['z'=16,'x'=4,'y'=4,'core'=2] {'x','y'}, dimensions={0} | all-to-all | bytes 524288 | tf_op jit(solution)/shard_map/all_to_all | solution.py:227
  49.7 0.0 copy-start.2
  49.7 5.2 %all-gather.1 = bf16[32,32,256]{2,1,0:T(8,128)(2,1)S(1)} all-gather(bf16[16,32,256]{2,1,0:T(8,128)(2,1)S(1)} %all_to_all.21), channel_id=3, replica_groups=mesh['z'=16,'x'=4,'y'=4,'core'=2] {'core'}, dimensions={0}, use_global_device_ids=true | all-gather | bytes 786432 | tf_op jit(solution)/shard_map/all_gather | solution.py:228
  54.8 0.0 copy-done.1
  54.8 0.0 copy-done
  54.8 0.0 copy-done.2
  54.8 0.8 expert.1
  55.7 2.2 %all-gather.2 = bf16[32,32,256]{2,1,0:T(8,128)(2,1)S(1)} all-gather(bf16[16,32,256]{2,1,0:T(8,128)(2,1)S(1)} %get-tuple-element.14), channel_id=4, replica_groups=mesh['z'=16,'x'=4,'y'=4,'core'=2] {'core'}, dimensions={0}, use_global_device_ids=true | all-gather | bytes 786432 | tf_op jit(solution)/shard_map/all_gather | solution.py:230
  57.9 0.1 fusion
  58.0 10.7 %all_to_all.22 = bf16[16,32,256]{2,1,0:T(8,128)(2,1)S(1)} all-to-all(bf16[16,32,256]{2,1,0:T(8,128)(2,1)S(1)} %fusion), channel_id=1, replica_groups=mesh['z'=16,'x'=4,'y'=4,'core'=2] {'x','y'}, dimensions={0} | all-to-all | bytes 524288 | tf_op jit(solution)/shard_map/all_to_all | solution.py:233
  68.8 13.8 %all_to_all.23 = bf16[16,2,256]{2,1,0:T(2,128)(2,1)S(1)} all-to-all(bf16[16,2,256]{2,1,0:T(2,128)(2,1)S(1)} %add_convert_fusion), channel_id=1, replica_groups=mesh['z'=16,'x'=4,'y'=4,'core'=2] {'z'}, dimensions={0} | all-to-all | bytes 32768 | tf_op jit(solution)/shard_map/all_to_all | solution.py:235
  82.6 0.8 convolution_convert_fusion.1
  (10 shorter events, 0.2 us)
Async XLA Ops:
  10.4 44.5 %copy-start.1 = (bf16[1,256,2048]{2,1,0:T(8,128)(2,1)S(1)}, bf16[1,256,2048]{2,1,0:T(8,128)(2,1)}, u32[]{:S(2)}) copy-start(bf16[1,256,2048]{2,1,0:T(8,128)(2,1)} %param.23) | copy-start | bytes 3145732
  10.4 44.4 %copy-start = (bf16[1,2048,256]{2,1,0:T(8,128)(2,1)S(1)}, bf16[1,2048,256]{2,1,0:T(8,128)(2,1)}, u32[]{:S(2)}) copy-start(bf16[1,2048,256]{2,1,0:T(8,128)(2,1)} %param.22) | copy-start | bytes 3145732
  49.7 5.2 %copy-start.2 = (f32[2048]{0:T(1024)S(1)}, f32[2048]{0:T(1024)}, u32[]{:S(2)}) copy-start(f32[2048]{0:T(1024)} %param.19) | copy-start | bytes 24580

commit v7 on v6

--- a/solution.py
+++ b/solution.py
@@ -217,11 +217,10 @@
     given = lax.all_gather(give, "core", axis=0)
     chip = keep + lax.dynamic_index_in_dim(given, 1 - core, 0, keepdims=False)
     chip = chip.astype(bf16).reshape(count, n_y, width)
-    packed = jnp.einsum("sr,ryc->syc", table, chip, preferred_element_type=f32)
-    packed = packed.astype(bf16).reshape(n_z, SLOTS, n_y, width).transpose(0, 2, 1, 3)
-    packed = packed.reshape(n_z * n_y, SLOTS, width)
-    got = lax.all_to_all(packed, ("z", "y"), split_axis=0, concat_axis=0, tiled=True)
-    hidden = jnp.sum(got.reshape(n_z, n_y, SLOTS, width).astype(f32), axis=1).reshape(slots, width)
+    packed = jnp.einsum("sr,ryc->ysc", table, chip, preferred_element_type=f32)
+    packed = packed.astype(bf16).reshape(n_y * n_z, SLOTS, width)
+    got = lax.all_to_all(packed, ("y", "z"), split_axis=0, concat_axis=0, tiled=True)
+    hidden = jnp.sum(got.reshape(n_y, slots, width).astype(f32), axis=0)
 
     spread = jnp.broadcast_to(hidden.astype(bf16)[None], (n_x * n_y, slots, width))
     plane = lax.all_to_all(spread, ("x", "y"), split_axis=0, concat_axis=0, tiled=True)

time: 84.2 us -> 84.1 us (level)
  no operation moved by 1% of the time
where the time goes in v7:
time: 84.1 us; the launch traced here: 83.3 us
  blocking collectives  79.4 us (94%)
  Pallas kernels  2.64 us (3%)
  matrix products  0.92 us (1%)
    all_to_all x1, blocking collectives, on_device(): lax.all_to_all(packed, ('y', 'z'), split_axis=0, concat_axis=0, tiled=True)  26.5 us
    all_to_all x1, blocking collectives, on_device(): lax.all_to_all(mixed.reshape(n_z, SLOTS, width), 'z', split_axis=0, conca...  13.8 us
    all_to_all x1, blocking collectives, on_device(): lax.all_to_all(spread, ('x', 'y'), split_axis=0, concat_axis=0, tiled=True)  12.7 us
    all_to_all x1, blocking collectives, on_device(): lax.all_to_all(half, ('x', 'y'), split_axis=0, concat_axis=0, tiled=True)  10.7 us
    all_gather x2, blocking collectives, on_device(): given = lax.all_gather(give, 'core', axis=0)  10.6 us
    all_gather x1, blocking collectives, on_device(): pair = lax.all_gather(plane, 'core', axis=0)  5.04 us
    pallas_call x1, Pallas kernels, attend(): pl.pallas_call(functools.partial(attend_kernel, n_y), out_shape=(half, ha...  1.82 us

profile of v7, /device:TPU:1, one launch (start us, length us, event | category | flops | bytes accessed | tf_op | source)
XLA Modules:
  0.0 83.3 jit_solution(6846862816191296623)
XLA Ops:
  0.0 1.8 %attend.1 = (f32[8,1024]{1,0:T(8,128)S(1)}, f32[8,1024]{1,0:T(8,128)S(1)}, bf16[32,8]{1,0:T(8,128)(2,1)S(1)}) custom-call(s32[8]{0:T(128)} %refs_0_.1, s32[8]{0:T(128)} %bitcast.34, bf16[8,256]{1,0:T(8,128)(2,1)} %refs_2_.1, bf16[512,256]{1,0:T(8,128)(2,1)} %bitcast.30, bf16[8,256]{1,0:T(8,128)(2,1)} %refs_4_.1, bf16[512,256]{1,0:T(8,128)(2,1)} %bitcast.31, ...), custom_call_target="tpu_custom_call" | custom-call | tf_op jit(solution)/shard_map/attend/pallas_call | solution.py:123
  1.8 8.4 %all-gather = f32[16,1024]{1,0:T(8,128)S(1)} all-gather(f32[8,1024]{1,0:T(8,128)S(1)} %get-tuple-element.12), channel_id=2, replica_groups=mesh['z'=16,'x'=4,'y'=4,'core'=2] {'core'}, dimensions={0}, use_global_device_ids=true | all-gather | bytes 98304 | tf_op jit(solution)/shard_map/all_gather | solution.py:217
  10.2 0.1 fusion
  10.4 0.0 copy-start
  10.4 0.0 copy-start.1
  10.4 26.5 %all_to_all.20 = bf16[64,2,256]{2,1,0:T(2,128)(2,1)S(1)} all-to-all(bf16[64,2,256]{2,1,0:T(2,128)(2,1)S(1)} %reshape.31), channel_id=1, replica_groups=mesh['z'=16,'x'=4,'y'=4,'core'=2] {'y','z'}, dimensions={0} | all-to-all | bytes 131072 | tf_op jit(solution)/shard_map/all_to_all | solution.py:222
  37.0 12.7 %all_to_all.21 = bf16[16,32,256]{2,1,0:T(8,128)(2,1)S(1)} all-to-all(bf16[16,32,256]{2,1,0:T(8,128)(2,1)S(1)} %broadcast_in_dim.4), channel_id=1, replica_groups=mesh['z'=16,'x'=4,'y'=4,'core'=2] {'x','y'}, dimensions={0} | all-to-all | bytes 524288 | tf_op jit(solution)/shard_map/all_to_all | solution.py:226
  49.7 0.0 copy-start.2
  49.7 5.0 %all-gather.1 = bf16[32,32,256]{2,1,0:T(8,128)(2,1)S(1)} all-gather(bf16[16,32,256]{2,1,0:T(8,128)(2,1)S(1)} %all_to_all.21), channel_id=3, replica_groups=mesh['z'=16,'x'=4,'y'=4,'core'=2] {'core'}, dimensions={0}, use_global_device_ids=true | all-gather | bytes 786432 | tf_op jit(solution)/shard_map/all_gather | solution.py:227
  54.7 0.0 copy-done
  54.7 0.0 copy-done.1
  54.7 0.0 copy-done.2
  54.7 0.8 expert.1
  55.6 2.2 %all-gather.2 = bf16[32,32,256]{2,1,0:T(8,128)(2,1)S(1)} all-gather(bf16[16,32,256]{2,1,0:T(8,128)(2,1)S(1)} %get-tuple-element.14), channel_id=4, replica_groups=mesh['z'=16,'x'=4,'y'=4,'core'=2] {'core'}, dimensions={0}, use_global_device_ids=true | all-gather | bytes 786432 | tf_op jit(solution)/shard_map/all_gather | solution.py:229
  57.8 0.1 fusion.1
  57.9 10.7 %all_to_all.22 = bf16[16,32,256]{2,1,0:T(8,128)(2,1)S(1)} all-to-all(bf16[16,32,256]{2,1,0:T(8,128)(2,1)S(1)} %fusion.1), channel_id=1, replica_groups=mesh['z'=16,'x'=4,'y'=4,'core'=2] {'x','y'}, dimensions={0} | all-to-all | bytes 524288 | tf_op jit(solution)/shard_map/all_to_all | solution.py:232
  68.7 13.8 %all_to_all.23 = bf16[16,2,256]{2,1,0:T(2,128)(2,1)S(1)} all-to-all(bf16[16,2,256]{2,1,0:T(2,128)(2,1)S(1)} %convert_element_type.55), channel_id=1, replica_groups=mesh['z'=16,'x'=4,'y'=4,'core'=2] {'z'}, dimensions={0} | all-to-all | bytes 32768 | tf_op jit(solution)/shard_map/all_to_all | solution.py:234
  82.5 0.8 convolution_convert_fusion.1
  (10 shorter events, 0.2 us)
Async XLA Ops:
  10.4 44.3 %copy-start = (bf16[1,2048,256]{2,1,0:T(8,128)(2,1)S(1)}, bf16[1,2048,256]{2,1,0:T(8,128)(2,1)}, u32[]{:S(2)}) copy-start(bf16[1,2048,256]{2,1,0:T(8,128)(2,1)} %param.22) | copy-start | bytes 3145732
  10.4 44.3 %copy-start.1 = (bf16[1,256,2048]{2,1,0:T(8,128)(2,1)S(1)}, bf16[1,256,2048]{2,1,0:T(8,128)(2,1)}, u32[]{:S(2)}) copy-start(bf16[1,256,2048]{2,1,0:T(8,128)(2,1)} %param.23) | copy-start | bytes 3145732
  49.7 5.0 %copy-start.2 = (f32[2048]{0:T(1024)S(1)}, f32[2048]{0:T(1024)}, u32[]{:S(2)}) copy-start(f32[2048]{0:T(1024)} %param.19) | copy-start | bytes 24580

commit v8 on v7

--- a/solution.py
+++ b/solution.py
@@ -20,7 +20,7 @@
 
 def attend_kernel(n_y, *refs):
     f32, bf16 = jnp.float32, jnp.bfloat16
-    sources, (keep, give, table), held, sems = refs[:9], refs[9:12], refs[12:21], refs[21]
+    sources, (keep, give, table, mask), held, sems = refs[:9], refs[9:13], refs[13:22], refs[22]
     core, my_y = lax.axis_index("core"), lax.axis_index("y")
     copies = [
         pltpu.make_async_copy(source, target, sems.at[i])
@@ -50,6 +50,7 @@
             place = place + (ids[q] == ids[r]).astype(jnp.int32)
         hot = jnp.where((name == r) & (slot == place), 1.0, hot)
     table[...] = hot.astype(bf16)
+    mask[...] = hot
     for copy in copies[2:5]:
         copy.wait()
     probs = []
@@ -122,9 +123,14 @@
     spaces = [pltpu.SMEM] * 2 + [pltpu.VMEM] * 7
     return pl.pallas_call(
         functools.partial(attend_kernel, n_y),
-        out_shape=(half, half, in_vmem((slots, count), jnp.bfloat16)),
+        out_shape=(
+            half,
+            half,
+            in_vmem((slots, count), jnp.bfloat16),
+            in_vmem((slots, count), jnp.float32),
+        ),
         in_specs=[anywhere] * len(args),
-        out_specs=(vmem,) * 3,
+        out_specs=(vmem,) * 4,
         scratch_shapes=[space(arg.shape, arg.dtype) for space, arg in zip(spaces, args)]
         + [pltpu.SemaphoreType.DMA((len(args),))],
         name="attend",
@@ -201,7 +207,7 @@
     core = lax.axis_index("core")
 
     slots = n_z * SLOTS
-    keep, give, table = attend(
+    keep, give, table, mask = attend(
         n_y,
         slots,
         queries,
@@ -234,9 +240,8 @@
     back = lax.all_to_all(
         mixed.reshape(n_z, SLOTS, width), "z", split_axis=0, concat_axis=0, tiled=True
     )
-    back = back.reshape(slots, width)
-    out = jnp.einsum("sr,sc->rc", table, back, preferred_element_type=f32)
-    return out.astype(bf16)
+    back = back.reshape(slots, 1, width).astype(f32)
+    return jnp.sum(mask[:, :, None] * back, axis=0).astype(bf16)
 
 
 def solution(mesh):

time: 84.1 us -> 84 us (level)
  no operation moved by 1% of the time
where the time goes in v8:
time: 84 us; the launch traced here: 83.2 us
  blocking collectives  79.4 us (95%)
  Pallas kernels  2.64 us (3%)
  other arithmetic  0.86 us (1%)
    all_to_all x1, blocking collectives, on_device(): lax.all_to_all(packed, ('y', 'z'), split_axis=0, concat_axis=0, tiled=True)  26.5 us
    all_to_all x1, blocking collectives, on_device(): lax.all_to_all(mixed.reshape(n_z, SLOTS, width), 'z', split_axis=0, conca...  13.8 us
    all_to_all x1, blocking collectives, on_device(): lax.all_to_all(spread, ('x', 'y'), split_axis=0, concat_axis=0, tiled=True)  12.7 us
    all_to_all x1, blocking collectives, on_device(): lax.all_to_all(half, ('x', 'y'), split_axis=0, concat_axis=0, tiled=True)  10.7 us
    all_gather x2, blocking collectives, on_device(): given = lax.all_gather(give, 'core', axis=0)  10.6 us
    all_gather x1, blocking collectives, on_device(): pair = lax.all_gather(plane, 'core', axis=0)  5.04 us
    pallas_call x1, Pallas kernels, attend(): pl.pallas_call(functools.partial(attend_kernel, n_y), out_shape=(half, ha...  1.82 us

profile of v8, /device:TPU:1, one launch (start us, length us, event | category | flops | bytes accessed | tf_op | source)
XLA Modules:
  0.0 83.2 jit_solution(936476228503112021)
XLA Ops:
  0.0 1.8 %attend.1 = (f32[8,1024]{1,0:T(8,128)S(1)}, f32[8,1024]{1,0:T(8,128)S(1)}, bf16[32,8]{1,0:T(8,128)(2,1)S(1)}, f32[32,8]{1,0:T(8,128)S(1)}) custom-call(s32[8]{0:T(128)} %refs_0_.1, s32[8]{0:T(128)} %bitcast.32, bf16[8,256]{1,0:T(8,128)(2,1)} %refs_2_.1, bf16[512,256]{1,0:T(8,128)(2,1)} %bitcast.28, bf16[8,256]{1,0:T(8,128)(2,1)} %refs_4_.1, ...), custom_call_target="tpu_custom_call" | custom-call | tf_op jit(solution)/shard_map/attend/pallas_call | solution.py:124
  1.8 8.4 %all-gather = f32[16,1024]{1,0:T(8,128)S(1)} all-gather(f32[8,1024]{1,0:T(8,128)S(1)} %get-tuple-element.13), channel_id=2, replica_groups=mesh['z'=16,'x'=4,'y'=4,'core'=2] {'core'}, dimensions={0}, use_global_device_ids=true | all-gather | bytes 98304 | tf_op jit(solution)/shard_map/all_gather | solution.py:223
  10.2 0.1 fusion
  10.4 0.0 copy-start
  10.4 0.0 copy-start.1
  10.4 26.5 %all_to_all.20 = bf16[64,2,256]{2,1,0:T(2,128)(2,1)S(1)} all-to-all(bf16[64,2,256]{2,1,0:T(2,128)(2,1)S(1)} %reshape.39), channel_id=1, replica_groups=mesh['z'=16,'x'=4,'y'=4,'core'=2] {'y','z'}, dimensions={0} | all-to-all | bytes 131072 | tf_op jit(solution)/shard_map/all_to_all | solution.py:228
  37.0 12.7 %all_to_all.21 = bf16[16,32,256]{2,1,0:T(8,128)(2,1)S(1)} all-to-all(bf16[16,32,256]{2,1,0:T(8,128)(2,1)S(1)} %broadcast_in_dim.4), channel_id=1, replica_groups=mesh['z'=16,'x'=4,'y'=4,'core'=2] {'x','y'}, dimensions={0} | all-to-all | bytes 524288 | tf_op jit(solution)/shard_map/all_to_all | solution.py:232
  49.7 0.0 copy-start.2
  49.7 5.0 %all-gather.1 = bf16[32,32,256]{2,1,0:T(8,128)(2,1)S(1)} all-gather(bf16[16,32,256]{2,1,0:T(8,128)(2,1)S(1)} %all_to_all.21), channel_id=3, replica_groups=mesh['z'=16,'x'=4,'y'=4,'core'=2] {'core'}, dimensions={0}, use_global_device_ids=true | all-gather | bytes 786432 | tf_op jit(solution)/shard_map/all_gather | solution.py:233
  54.7 0.0 copy-done
  54.7 0.0 copy-done.1
  54.7 0.0 copy-done.2
  54.7 0.8 expert.1
  55.6 2.2 %all-gather.2 = bf16[32,32,256]{2,1,0:T(8,128)(2,1)S(1)} all-gather(bf16[16,32,256]{2,1,0:T(8,128)(2,1)S(1)} %get-tuple-element.16), channel_id=4, replica_groups=mesh['z'=16,'x'=4,'y'=4,'core'=2] {'core'}, dimensions={0}, use_global_device_ids=true | all-gather | bytes 786432 | tf_op jit(solution)/shard_map/all_gather | solution.py:235
  57.8 0.1 fusion.1
  57.9 10.7 %all_to_all.22 = bf16[16,32,256]{2,1,0:T(8,128)(2,1)S(1)} all-to-all(bf16[16,32,256]{2,1,0:T(8,128)(2,1)S(1)} %fusion.1), channel_id=1, replica_groups=mesh['z'=16,'x'=4,'y'=4,'core'=2] {'x','y'}, dimensions={0} | all-to-all | bytes 524288 | tf_op jit(solution)/shard_map/all_to_all | solution.py:238
  68.7 13.8 %all_to_all.23 = bf16[16,2,256]{2,1,0:T(2,128)(2,1)S(1)} all-to-all(bf16[16,2,256]{2,1,0:T(2,128)(2,1)S(1)} %convert_element_type.66), channel_id=1, replica_groups=mesh['z'=16,'x'=4,'y'=4,'core'=2] {'z'}, dimensions={0} | all-to-all | bytes 32768 | tf_op jit(solution)/shard_map/all_to_all | solution.py:240
  82.5 0.7 multiply_reduce_fusion
  (10 shorter events, 0.2 us)
Async XLA Ops:
  10.4 44.3 %copy-start = (bf16[1,2048,256]{2,1,0:T(8,128)(2,1)S(1)}, bf16[1,2048,256]{2,1,0:T(8,128)(2,1)}, u32[]{:S(2)}) copy-start(bf16[1,2048,256]{2,1,0:T(8,128)(2,1)} %param.22) | copy-start | bytes 3145732
  10.4 44.3 %copy-start.1 = (bf16[1,256,2048]{2,1,0:T(8,128)(2,1)S(1)}, bf16[1,256,2048]{2,1,0:T(8,128)(2,1)}, u32[]{:S(2)}) copy-start(bf16[1,256,2048]{2,1,0:T(8,128)(2,1)} %param.23) | copy-start | bytes 3145732
  49.7 5.0 %copy-start.2 = (f32[2048]{0:T(1024)S(1)}, f32[2048]{0:T(1024)}, u32[]{:S(2)}) copy-start(f32[2048]{0:T(1024)} %param.19) | copy-start | bytes 24580

commit v9 on v8

--- a/solution.py
+++ b/solution.py
@@ -148,7 +148,7 @@
     for y in range(n_y):
         for c in range(CORES):
             cols = pl.ds((y * CORES + c) * width, width)
-            block = [pair[c, x * n_y + y] for x in range(n_x)]
+            block = [pair[c, y * n_x + x] for x in range(n_x)]
             block = jnp.concatenate(block, axis=0).astype(f32)
             squares = squares + block * block
             scaled = (block * gain[:, cols]).astype(bf16)
@@ -164,8 +164,8 @@
         own = jnp.where(core == 0, both[0], both[1])
         other = jnp.where(core == 0, both[1], both[0]).astype(bf16)
         for x in range(n_x):
-            keep[x * n_y + y] = own[x * slots : (x + 1) * slots]
-            give[x * n_y + y] = other[x * slots : (x + 1) * slots]
+            keep[y * n_x + x] = own[x * slots : (x + 1) * slots]
+            give[y * n_x + x] = other[x * slots : (x + 1) * slots]
 
 
 def run_expert(n_x, n_y, pair, norm_gain, w_up, w_down):
@@ -228,14 +228,14 @@
     got = lax.all_to_all(packed, ("y", "z"), split_axis=0, concat_axis=0, tiled=True)
     hidden = jnp.sum(got.reshape(n_y, slots, width).astype(f32), axis=0)
 
-    spread = jnp.broadcast_to(hidden.astype(bf16)[None], (n_x * n_y, slots, width))
-    plane = lax.all_to_all(spread, ("x", "y"), split_axis=0, concat_axis=0, tiled=True)
+    spread = jnp.broadcast_to(hidden.astype(bf16)[None], (n_y * n_x, slots, width))
+    plane = lax.all_to_all(spread, ("y", "x"), split_axis=0, concat_axis=0, tiled=True)
     pair = lax.all_gather(plane, "core", axis=0)
     keep, give = run_expert(n_x, n_y, pair, norm_gain, w_up[0], w_down[0])
     given = lax.all_gather(give, "core", axis=0)
     half = keep + lax.dynamic_index_in_dim(given, 1 - core, 0, keepdims=False).astype(f32)
     half = half.astype(bf16)
-    parts = lax.all_to_all(half, ("x", "y"), split_axis=0, concat_axis=0, tiled=True)
+    parts = lax.all_to_all(half, ("y", "x"), split_axis=0, concat_axis=0, tiled=True)
     mixed = (hidden + jnp.sum(parts.astype(f32), axis=0)).astype(bf16)
     back = lax.all_to_all(
         mixed.reshape(n_z, SLOTS, width), "z", split_axis=0, concat_axis=0, tiled=True

time: 84 us -> 84 us (level)
  no operation moved by 1% of the time
where the time goes in v9:
time: 84 us; the launch traced here: 83.4 us
  blocking collectives  79.6 us (95%)
  Pallas kernels  2.64 us (3%)
  other arithmetic  0.86 us (1%)
    all_to_all x1, blocking collectives, on_device(): lax.all_to_all(packed, ('y', 'z'), split_axis=0, concat_axis=0, tiled=True)  26.5 us
    all_to_all x1, blocking collectives, on_device(): lax.all_to_all(mixed.reshape(n_z, SLOTS, width), 'z', split_axis=0, conca...  13.8 us
    all_to_all x1, blocking collectives, on_device(): lax.all_to_all(spread, ('y', 'x'), split_axis=0, concat_axis=0, tiled=True)  12.8 us
    all_to_all x1, blocking collectives, on_device(): lax.all_to_all(half, ('y', 'x'), split_axis=0, concat_axis=0, tiled=True)  10.7 us
    all_gather x2, blocking collectives, on_device(): given = lax.all_gather(give, 'core', axis=0)  10.6 us
    all_gather x1, blocking collectives, on_device(): pair = lax.all_gather(plane, 'core', axis=0)  5.08 us
    pallas_call x1, Pallas kernels, attend(): pl.pallas_call(functools.partial(attend_kernel, n_y), out_shape=(half, ha...  1.82 us

profile of v9, /device:TPU:1, one launch (start us, length us, event | category | flops | bytes accessed | tf_op | source)
XLA Modules:
  0.0 83.4 jit_solution(3879289517508364576)
XLA Ops:
  0.0 1.8 %attend.1 = (f32[8,1024]{1,0:T(8,128)S(1)}, f32[8,1024]{1,0:T(8,128)S(1)}, bf16[32,8]{1,0:T(8,128)(2,1)S(1)}, f32[32,8]{1,0:T(8,128)S(1)}) custom-call(s32[8]{0:T(128)} %refs_0_.1, s32[8]{0:T(128)} %bitcast.32, bf16[8,256]{1,0:T(8,128)(2,1)} %refs_2_.1, bf16[512,256]{1,0:T(8,128)(2,1)} %bitcast.28, bf16[8,256]{1,0:T(8,128)(2,1)} %refs_4_.1, ...), custom_call_target="tpu_custom_call" | custom-call | tf_op jit(solution)/shard_map/attend/pallas_call | solution.py:124
  1.8 8.4 %all-gather = f32[16,1024]{1,0:T(8,128)S(1)} all-gather(f32[8,1024]{1,0:T(8,128)S(1)} %get-tuple-element.13), channel_id=2, replica_groups=mesh['z'=16,'x'=4,'y'=4,'core'=2] {'core'}, dimensions={0}, use_global_device_ids=true | all-gather | bytes 98304 | tf_op jit(solution)/shard_map/all_gather | solution.py:223
  10.2 0.1 fusion
  10.4 0.0 copy-start
  10.4 0.0 copy-start.1
  10.4 26.5 %all_to_all.20 = bf16[64,2,256]{2,1,0:T(2,128)(2,1)S(1)} all-to-all(bf16[64,2,256]{2,1,0:T(2,128)(2,1)S(1)} %reshape.39), channel_id=1, replica_groups=mesh['z'=16,'x'=4,'y'=4,'core'=2] {'y','z'}, dimensions={0} | all-to-all | bytes 131072 | tf_op jit(solution)/shard_map/all_to_all | solution.py:228
  37.0 12.8 %all_to_all.21 = bf16[16,32,256]{2,1,0:T(8,128)(2,1)S(1)} all-to-all(bf16[16,32,256]{2,1,0:T(8,128)(2,1)S(1)} %broadcast_in_dim.4), channel_id=1, replica_groups=mesh['z'=16,'x'=4,'y'=4,'core'=2] {'y','x'}, dimensions={0} | all-to-all | bytes 524288 | tf_op jit(solution)/shard_map/all_to_all | solution.py:232
  49.9 0.0 copy-start.2
  49.9 5.1 %all-gather.1 = bf16[32,32,256]{2,1,0:T(8,128)(2,1)S(1)} all-gather(bf16[16,32,256]{2,1,0:T(8,128)(2,1)S(1)} %all_to_all.21), channel_id=3, replica_groups=mesh['z'=16,'x'=4,'y'=4,'core'=2] {'core'}, dimensions={0}, use_global_device_ids=true | all-gather | bytes 786432 | tf_op jit(solution)/shard_map/all_gather | solution.py:233
  55.0 0.0 copy-done
  55.0 0.0 copy-done.1
  55.0 0.0 copy-done.2
  55.0 0.8 expert.1
  55.8 2.2 %all-gather.2 = bf16[32,32,256]{2,1,0:T(8,128)(2,1)S(1)} all-gather(bf16[16,32,256]{2,1,0:T(8,128)(2,1)S(1)} %get-tuple-element.16), channel_id=4, replica_groups=mesh['z'=16,'x'=4,'y'=4,'core'=2] {'core'}, dimensions={0}, use_global_device_ids=true | all-gather | bytes 786432 | tf_op jit(solution)/shard_map/all_gather | solution.py:235
  58.0 0.1 fusion.1
  58.1 10.7 %all_to_all.22 = bf16[16,32,256]{2,1,0:T(8,128)(2,1)S(1)} all-to-all(bf16[16,32,256]{2,1,0:T(8,128)(2,1)S(1)} %fusion.1), channel_id=1, replica_groups=mesh['z'=16,'x'=4,'y'=4,'core'=2] {'y','x'}, dimensions={0} | all-to-all | bytes 524288 | tf_op jit(solution)/shard_map/all_to_all | solution.py:238
  68.9 13.8 %all_to_all.23 = bf16[16,2,256]{2,1,0:T(2,128)(2,1)S(1)} all-to-all(bf16[16,2,256]{2,1,0:T(2,128)(2,1)S(1)} %convert_element_type.66), channel_id=1, replica_groups=mesh['z'=16,'x'=4,'y'=4,'core'=2] {'z'}, dimensions={0} | all-to-all | bytes 32768 | tf_op jit(solution)/shard_map/all_to_all | solution.py:240
  82.7 0.7 multiply_reduce_fusion
  (10 shorter events, 0.2 us)
Async XLA Ops:
  10.4 44.6 %copy-start = (bf16[1,2048,256]{2,1,0:T(8,128)(2,1)S(1)}, bf16[1,2048,256]{2,1,0:T(8,128)(2,1)}, u32[]{:S(2)}) copy-start(bf16[1,2048,256]{2,1,0:T(8,128)(2,1)} %param.22) | copy-start | bytes 3145732
  10.4 44.5 %copy-start.1 = (bf16[1,256,2048]{2,1,0:T(8,128)(2,1)S(1)}, bf16[1,256,2048]{2,1,0:T(8,128)(2,1)}, u32[]{:S(2)}) copy-start(bf16[1,256,2048]{2,1,0:T(8,128)(2,1)} %param.23) | copy-start | bytes 3145732
  49.9 5.1 %copy-start.2 = (f32[2048]{0:T(1024)S(1)}, f32[2048]{0:T(1024)}, u32[]{:S(2)}) copy-start(f32[2048]{0:T(1024)} %param.19) | copy-start | bytes 24580

commit v10 on v9

--- a/solution.py
+++ b/solution.py
@@ -148,7 +148,7 @@
     for y in range(n_y):
         for c in range(CORES):
             cols = pl.ds((y * CORES + c) * width, width)
-            block = [pair[c, y * n_x + x] for x in range(n_x)]
+            block = [pair[c, x * n_y + y] for x in range(n_x)]
             block = jnp.concatenate(block, axis=0).astype(f32)
             squares = squares + block * block
             scaled = (block * gain[:, cols]).astype(bf16)
@@ -228,8 +228,8 @@
     got = lax.all_to_all(packed, ("y", "z"), split_axis=0, concat_axis=0, tiled=True)
     hidden = jnp.sum(got.reshape(n_y, slots, width).astype(f32), axis=0)
 
-    spread = jnp.broadcast_to(hidden.astype(bf16)[None], (n_y * n_x, slots, width))
-    plane = lax.all_to_all(spread, ("y", "x"), split_axis=0, concat_axis=0, tiled=True)
+    spread = jnp.broadcast_to(hidden.astype(bf16)[None], (n_x * n_y, slots, width))
+    plane = lax.all_to_all(spread, ("x", "y"), split_axis=0, concat_axis=0, tiled=True)
     pair = lax.all_gather(plane, "core", axis=0)
     keep, give = run_expert(n_x, n_y, pair, norm_gain, w_up[0], w_down[0])
     given = lax.all_gather(give, "core", axis=0)

time: 84 us -> 84.3 us (level)
  no operation moved by 1% of the time
where the time goes in v10:
time: 84.3 us; the launch traced here: 83.8 us
  blocking collectives  79.9 us (95%)
  Pallas kernels  2.64 us (3%)
  other arithmetic  0.86 us (1%)
    all_to_all x1, blocking collectives, on_device(): lax.all_to_all(packed, ('y', 'z'), split_axis=0, concat_axis=0, tiled=True)  26.5 us
    all_to_all x1, blocking collectives, on_device(): lax.all_to_all(mixed.reshape(n_z, SLOTS, width), 'z', split_axis=0, conca...  13.8 us
    all_to_all x1, blocking collectives, on_device(): lax.all_to_all(spread, ('x', 'y'), split_axis=0, concat_axis=0, tiled=True)  12.7 us
    all_to_all x1, blocking collectives, on_device(): lax.all_to_all(half, ('y', 'x'), split_axis=0, concat_axis=0, tiled=True)  11.3 us
    all_gather x2, blocking collectives, on_device(): given = lax.all_gather(give, 'core', axis=0)  10.6 us
    all_gather x1, blocking collectives, on_device(): pair = lax.all_gather(plane, 'core', axis=0)  5.04 us
    pallas_call x1, Pallas kernels, attend(): pl.pallas_call(functools.partial(attend_kernel, n_y), out_shape=(half, ha...  1.82 us

profile of v10, /device:TPU:1, one launch (start us, length us, event | category | flops | bytes accessed | tf_op | source)
XLA Modules:
  0.0 83.8 jit_solution(4751483577239059718)
XLA Ops:
  0.0 1.8 %attend.1 = (f32[8,1024]{1,0:T(8,128)S(1)}, f32[8,1024]{1,0:T(8,128)S(1)}, bf16[32,8]{1,0:T(8,128)(2,1)S(1)}, f32[32,8]{1,0:T(8,128)S(1)}) custom-call(s32[8]{0:T(128)} %refs_0_.1, s32[8]{0:T(128)} %bitcast.32, bf16[8,256]{1,0:T(8,128)(2,1)} %refs_2_.1, bf16[512,256]{1,0:T(8,128)(2,1)} %bitcast.28, bf16[8,256]{1,0:T(8,128)(2,1)} %refs_4_.1, ...), custom_call_target="tpu_custom_call" | custom-call | tf_op jit(solution)/shard_map/attend/pallas_call | solution.py:124
  1.8 8.4 %all-gather = f32[16,1024]{1,0:T(8,128)S(1)} all-gather(f32[8,1024]{1,0:T(8,128)S(1)} %get-tuple-element.13), channel_id=2, replica_groups=mesh['z'=16,'x'=4,'y'=4,'core'=2] {'core'}, dimensions={0}, use_global_device_ids=true | all-gather | bytes 98304 | tf_op jit(solution)/shard_map/all_gather | solution.py:223
  10.2 0.1 fusion
  10.4 0.0 copy-start
  10.4 0.0 copy-start.1
  10.4 26.5 %all_to_all.20 = bf16[64,2,256]{2,1,0:T(2,128)(2,1)S(1)} all-to-all(bf16[64,2,256]{2,1,0:T(2,128)(2,1)S(1)} %reshape.39), channel_id=1, replica_groups=mesh['z'=16,'x'=4,'y'=4,'core'=2] {'y','z'}, dimensions={0} | all-to-all | bytes 131072 | tf_op jit(solution)/shard_map/all_to_all | solution.py:228
  37.0 12.7 %all_to_all.21 = bf16[16,32,256]{2,1,0:T(8,128)(2,1)S(1)} all-to-all(bf16[16,32,256]{2,1,0:T(8,128)(2,1)S(1)} %broadcast_in_dim.4), channel_id=1, replica_groups=mesh['z'=16,'x'=4,'y'=4,'core'=2] {'x','y'}, dimensions={0} | all-to-all | bytes 524288 | tf_op jit(solution)/shard_map/all_to_all | solution.py:232
  49.7 0.0 copy-start.2
  49.7 5.0 %all-gather.1 = bf16[32,32,256]{2,1,0:T(8,128)(2,1)S(1)} all-gather(bf16[16,32,256]{2,1,0:T(8,128)(2,1)S(1)} %all_to_all.21), channel_id=3, replica_groups=mesh['z'=16,'x'=4,'y'=4,'core'=2] {'core'}, dimensions={0}, use_global_device_ids=true | all-gather | bytes 786432 | tf_op jit(solution)/shard_map/all_gather | solution.py:233
  54.7 0.0 copy-done
  54.7 0.0 copy-done.1
  54.7 0.0 copy-done.2
  54.7 0.8 expert.1
  55.6 2.2 %all-gather.2 = bf16[32,32,256]{2,1,0:T(8,128)(2,1)S(1)} all-gather(bf16[16,32,256]{2,1,0:T(8,128)(2,1)S(1)} %get-tuple-element.16), channel_id=4, replica_groups=mesh['z'=16,'x'=4,'y'=4,'core'=2] {'core'}, dimensions={0}, use_global_device_ids=true | all-gather | bytes 786432 | tf_op jit(solution)/shard_map/all_gather | solution.py:235
  57.8 0.1 fusion.1
  57.9 11.3 %all_to_all.22 = bf16[16,32,256]{2,1,0:T(8,128)(2,1)S(1)} all-to-all(bf16[16,32,256]{2,1,0:T(8,128)(2,1)S(1)} %fusion.1), channel_id=1, replica_groups=mesh['z'=16,'x'=4,'y'=4,'core'=2] {'y','x'}, dimensions={0} | all-to-all | bytes 524288 | tf_op jit(solution)/shard_map/all_to_all | solution.py:238
  69.2 13.8 %all_to_all.23 = bf16[16,2,256]{2,1,0:T(2,128)(2,1)S(1)} all-to-all(bf16[16,2,256]{2,1,0:T(2,128)(2,1)S(1)} %convert_element_type.66), channel_id=1, replica_groups=mesh['z'=16,'x'=4,'y'=4,'core'=2] {'z'}, dimensions={0} | all-to-all | bytes 32768 | tf_op jit(solution)/shard_map/all_to_all | solution.py:240
  83.1 0.7 multiply_reduce_fusion
  (10 shorter events, 0.2 us)
Async XLA Ops:
  10.4 44.3 %copy-start = (bf16[1,2048,256]{2,1,0:T(8,128)(2,1)S(1)}, bf16[1,2048,256]{2,1,0:T(8,128)(2,1)}, u32[]{:S(2)}) copy-start(bf16[1,2048,256]{2,1,0:T(8,128)(2,1)} %param.22) | copy-start | bytes 3145732
  10.4 44.3 %copy-start.1 = (bf16[1,256,2048]{2,1,0:T(8,128)(2,1)S(1)}, bf16[1,256,2048]{2,1,0:T(8,128)(2,1)}, u32[]{:S(2)}) copy-start(bf16[1,256,2048]{2,1,0:T(8,128)(2,1)} %param.23) | copy-start | bytes 3145732
  49.7 5.0 %copy-start.2 = (f32[2048]{0:T(1024)S(1)}, f32[2048]{0:T(1024)}, u32[]{:S(2)}) copy-start(f32[2048]{0:T(1024)} %param.19) | copy-start | bytes 24580

commit v11 on v9

--- a/solution.py
+++ b/solution.py
@@ -89,7 +89,8 @@
         high = resid[:, pl.ds((y * CORES + 1) * width, width)].astype(f32)
         rest = jnp.where(my_y == y, jnp.where(core == 0, low, high), 0.0)
         keep[:, pl.ds(y * width, width)] = jnp.where(core == 0, pair[0], pair[1]) + rest
-        give[:, pl.ds(y * width, width)] = jnp.where(core == 0, pair[1], pair[0])
+        given = jnp.where(core == 0, pair[1], pair[0])
+        give[:, pl.ds(y * width, width)] = given.astype(bf16)
 
 
 def attend(
@@ -118,14 +119,14 @@
         w_out,
         resid,
     )
-    half = in_vmem((count, w_out.shape[1] // CORES), jnp.float32)
+    shape = (count, w_out.shape[1] // CORES)
     vmem, anywhere = pl.BlockSpec(memory_space=pltpu.VMEM), pl.BlockSpec(memory_space=pl.ANY)
     spaces = [pltpu.SMEM] * 2 + [pltpu.VMEM] * 7
     return pl.pallas_call(
         functools.partial(attend_kernel, n_y),
         out_shape=(
-            half,
-            half,
+            in_vmem(shape, jnp.float32),
+            in_vmem(shape, jnp.bfloat16),
             in_vmem((slots, count), jnp.bfloat16),
             in_vmem((slots, count), jnp.float32),
         ),
@@ -221,7 +222,7 @@
         experts[:, 0],
     )
     given = lax.all_gather(give, "core", axis=0)
-    chip = keep + lax.dynamic_index_in_dim(given, 1 - core, 0, keepdims=False)
+    chip = keep + lax.dynamic_index_in_dim(given, 1 - core, 0, keepdims=False).astype(f32)
     chip = chip.astype(bf16).reshape(count, n_y, width)
     packed = jnp.einsum("sr,ryc->ysc", table, chip, preferred_element_type=f32)
     packed = packed.astype(bf16).reshape(n_y * n_z, SLOTS, width)

time: 84 us -> 84 us (level)
  no operation moved by 1% of the time
where the time goes in v11:
time: 84 us; the launch traced here: 83.4 us
  blocking collectives  79.5 us (95%)
  Pallas kernels  2.64 us (3%)
  other arithmetic  0.86 us (1%)
    all_to_all x1, blocking collectives, on_device(): lax.all_to_all(packed, ('y', 'z'), split_axis=0, concat_axis=0, tiled=True)  26.5 us
    all_to_all x1, blocking collectives, on_device(): lax.all_to_all(mixed.reshape(n_z, SLOTS, width), 'z', split_axis=0, conca...  13.8 us
    all_to_all x1, blocking collectives, on_device(): lax.all_to_all(spread, ('y', 'x'), split_axis=0, concat_axis=0, tiled=True)  12.8 us
    all_to_all x1, blocking collectives, on_device(): lax.all_to_all(half, ('y', 'x'), split_axis=0, concat_axis=0, tiled=True)  10.7 us
    all_gather x2, blocking collectives, on_device(): given = lax.all_gather(give, 'core', axis=0)  10.6 us
    all_gather x1, blocking collectives, on_device(): pair = lax.all_gather(plane, 'core', axis=0)  5.07 us
    pallas_call x1, Pallas kernels, attend(): pl.pallas_call(functools.partial(attend_kernel, n_y), out_shape=(in_vmem(...  1.82 us

profile of v11, /device:TPU:1, one launch (start us, length us, event | category | flops | bytes accessed | tf_op | source)
XLA Modules:
  0.0 83.4 jit_solution(14012858718929840813)
XLA Ops:
  0.0 1.8 %attend.1 = (f32[8,1024]{1,0:T(8,128)S(1)}, bf16[8,1024]{1,0:T(8,128)(2,1)S(1)}, bf16[32,8]{1,0:T(8,128)(2,1)S(1)}, f32[32,8]{1,0:T(8,128)S(1)}) custom-call(s32[8]{0:T(128)} %refs_0_.1, s32[8]{0:T(128)} %bitcast.31, bf16[8,256]{1,0:T(8,128)(2,1)} %refs_2_.1, bf16[512,256]{1,0:T(8,128)(2,1)} %bitcast.27, bf16[8,256]{1,0:T(8,128)(2,1)} %refs_4_.1, ...), custom_call_target="tpu_custom_call" | custom-call | tf_op jit(solution)/shard_map/attend/pallas_call | solution.py:125
  1.8 8.4 %all-gather = bf16[16,1024]{1,0:T(8,128)(2,1)S(1)} all-gather(bf16[8,1024]{1,0:T(8,128)(2,1)S(1)} %get-tuple-element.13), channel_id=2, replica_groups=mesh['z'=16,'x'=4,'y'=4,'core'=2] {'core'}, dimensions={0}, use_global_device_ids=true | all-gather | bytes 49152 | tf_op jit(solution)/shard_map/all_gather | solution.py:224
  10.2 0.1 fusion
  10.4 0.0 copy-start
  10.4 0.0 copy-start.1
  10.4 26.5 %all_to_all.20 = bf16[64,2,256]{2,1,0:T(2,128)(2,1)S(1)} all-to-all(bf16[64,2,256]{2,1,0:T(2,128)(2,1)S(1)} %reshape.41), channel_id=1, replica_groups=mesh['z'=16,'x'=4,'y'=4,'core'=2] {'y','z'}, dimensions={0} | all-to-all | bytes 131072 | tf_op jit(solution)/shard_map/all_to_all | solution.py:229
  37.0 12.8 %all_to_all.21 = bf16[16,32,256]{2,1,0:T(8,128)(2,1)S(1)} all-to-all(bf16[16,32,256]{2,1,0:T(8,128)(2,1)S(1)} %broadcast_in_dim.4), channel_id=1, replica_groups=mesh['z'=16,'x'=4,'y'=4,'core'=2] {'y','x'}, dimensions={0} | all-to-all | bytes 524288 | tf_op jit(solution)/shard_map/all_to_all | solution.py:233
  49.9 0.0 copy-start.2
  49.9 5.1 %all-gather.1 = bf16[32,32,256]{2,1,0:T(8,128)(2,1)S(1)} all-gather(bf16[16,32,256]{2,1,0:T(8,128)(2,1)S(1)} %all_to_all.21), channel_id=3, replica_groups=mesh['z'=16,'x'=4,'y'=4,'core'=2] {'core'}, dimensions={0}, use_global_device_ids=true | all-gather | bytes 786432 | tf_op jit(solution)/shard_map/all_gather | solution.py:234
  54.9 0.0 copy-done
  54.9 0.0 copy-done.1
  54.9 0.0 copy-done.2
  54.9 0.8 expert.1
  55.8 2.2 %all-gather.2 = bf16[32,32,256]{2,1,0:T(8,128)(2,1)S(1)} all-gather(bf16[16,32,256]{2,1,0:T(8,128)(2,1)S(1)} %get-tuple-element.16), channel_id=4, replica_groups=mesh['z'=16,'x'=4,'y'=4,'core'=2] {'core'}, dimensions={0}, use_global_device_ids=true | all-gather | bytes 786432 | tf_op jit(solution)/shard_map/all_gather | solution.py:236
  58.0 0.1 fusion.1
  58.1 10.7 %all_to_all.22 = bf16[16,32,256]{2,1,0:T(8,128)(2,1)S(1)} all-to-all(bf16[16,32,256]{2,1,0:T(8,128)(2,1)S(1)} %fusion.1), channel_id=1, replica_groups=mesh['z'=16,'x'=4,'y'=4,'core'=2] {'y','x'}, dimensions={0} | all-to-all | bytes 524288 | tf_op jit(solution)/shard_map/all_to_all | solution.py:239
  68.9 13.8 %all_to_all.23 = bf16[16,2,256]{2,1,0:T(2,128)(2,1)S(1)} all-to-all(bf16[16,2,256]{2,1,0:T(2,128)(2,1)S(1)} %convert_element_type.74), channel_id=1, replica_groups=mesh['z'=16,'x'=4,'y'=4,'core'=2] {'z'}, dimensions={0} | all-to-all | bytes 32768 | tf_op jit(solution)/shard_map/all_to_all | solution.py:241
  82.7 0.7 multiply_reduce_fusion
  (10 shorter events, 0.2 us)
Async XLA Ops:
  10.4 44.6 %copy-start = (bf16[1,2048,256]{2,1,0:T(8,128)(2,1)S(1)}, bf16[1,2048,256]{2,1,0:T(8,128)(2,1)}, u32[]{:S(2)}) copy-start(bf16[1,2048,256]{2,1,0:T(8,128)(2,1)} %param.22) | copy-start | bytes 3145732
  10.4 44.5 %copy-start.1 = (bf16[1,256,2048]{2,1,0:T(8,128)(2,1)S(1)}, bf16[1,256,2048]{2,1,0:T(8,128)(2,1)}, u32[]{:S(2)}) copy-start(bf16[1,256,2048]{2,1,0:T(8,128)(2,1)} %param.23) | copy-start | bytes 3145732
  49.9 5.1 %copy-start.2 = (f32[2048]{0:T(1024)S(1)}, f32[2048]{0:T(1024)}, u32[]{:S(2)}) copy-start(f32[2048]{0:T(1024)} %param.19) | copy-start | bytes 24580

commit v12 on v8

--- a/solution.py
+++ b/solution.py
@@ -161,7 +161,7 @@
         for c in range(CORES):
             cols = pl.ds((y * CORES + c) * width, width)
             both.append(jnp.dot(act, down[:, cols], preferred_element_type=f32))
-        own = jnp.where(core == 0, both[0], both[1])
+        own = jnp.where(core == 0, both[0], both[1]).astype(bf16)
         other = jnp.where(core == 0, both[1], both[0]).astype(bf16)
         for x in range(n_x):
             keep[x * n_y + y] = own[x * slots : (x + 1) * slots]
@@ -177,7 +177,7 @@
     return pl.pallas_call(
         functools.partial(expert_kernel, n_x, n_y),
         out_shape=(
-            in_vmem(pair.shape[1:], jnp.float32),
+            in_vmem(pair.shape[1:], jnp.bfloat16),
             in_vmem(pair.shape[1:], jnp.bfloat16),
         ),
         in_specs=[vmem] * 4,
@@ -233,8 +233,8 @@
     pair = lax.all_gather(plane, "core", axis=0)
     keep, give = run_expert(n_x, n_y, pair, norm_gain, w_up[0], w_down[0])
     given = lax.all_gather(give, "core", axis=0)
-    half = keep + lax.dynamic_index_in_dim(given, 1 - core, 0, keepdims=False).astype(f32)
-    half = half.astype(bf16)
+    half = lax.dynamic_index_in_dim(given, 1 - core, 0, keepdims=False).astype(f32)
+    half = (keep.astype(f32) + half).astype(bf16)
     parts = lax.all_to_all(half, ("x", "y"), split_axis=0, concat_axis=0, tiled=True)
     mixed = (hidden + jnp.sum(parts.astype(f32), axis=0)).astype(bf16)
     back = lax.all_to_all(

time: 84 us -> 84 us (level)
  no operation moved by 1% of the time
where the time goes in v12:
time: 84 us; the launch traced here: 83.2 us
  blocking collectives  79.4 us (95%)
  Pallas kernels  2.64 us (3%)
  other arithmetic  0.86 us (1%)
    all_to_all x1, blocking collectives, on_device(): lax.all_to_all(packed, ('y', 'z'), split_axis=0, concat_axis=0, tiled=True)  26.5 us
    all_to_all x1, blocking collectives, on_device(): lax.all_to_all(mixed.reshape(n_z, SLOTS, width), 'z', split_axis=0, conca...  13.8 us
    all_to_all x1, blocking collectives, on_device(): lax.all_to_all(spread, ('x', 'y'), split_axis=0, concat_axis=0, tiled=True)  12.7 us
    all_to_all x1, blocking collectives, on_device(): lax.all_to_all(half, ('x', 'y'), split_axis=0, concat_axis=0, tiled=True)  10.7 us
    all_gather x2, blocking collectives, on_device(): given = lax.all_gather(give, 'core', axis=0)  10.6 us
    all_gather x1, blocking collectives, on_device(): pair = lax.all_gather(plane, 'core', axis=0)  5.04 us
    pallas_call x1, Pallas kernels, attend(): pl.pallas_call(functools.partial(attend_kernel, n_y), out_shape=(half, ha...  1.82 us

profile of v12, /device:TPU:1, one launch (start us, length us, event | category | flops | bytes accessed | tf_op | source)
XLA Modules:
  0.0 83.2 jit_solution(16087290299184574408)
XLA Ops:
  0.0 1.8 %attend.1 = (f32[8,1024]{1,0:T(8,128)S(1)}, f32[8,1024]{1,0:T(8,128)S(1)}, bf16[32,8]{1,0:T(8,128)(2,1)S(1)}, f32[32,8]{1,0:T(8,128)S(1)}) custom-call(s32[8]{0:T(128)} %refs_0_.1, s32[8]{0:T(128)} %bitcast.32, bf16[8,256]{1,0:T(8,128)(2,1)} %refs_2_.1, bf16[512,256]{1,0:T(8,128)(2,1)} %bitcast.28, bf16[8,256]{1,0:T(8,128)(2,1)} %refs_4_.1, ...), custom_call_target="tpu_custom_call" | custom-call | tf_op jit(solution)/shard_map/attend/pallas_call | solution.py:124
  1.8 8.4 %all-gather = f32[16,1024]{1,0:T(8,128)S(1)} all-gather(f32[8,1024]{1,0:T(8,128)S(1)} %get-tuple-element.13), channel_id=2, replica_groups=mesh['z'=16,'x'=4,'y'=4,'core'=2] {'core'}, dimensions={0}, use_global_device_ids=true | all-gather | bytes 98304 | tf_op jit(solution)/shard_map/all_gather | solution.py:223
  10.2 0.1 fusion
  10.4 0.0 copy-start
  10.4 0.0 copy-start.1
  10.4 26.5 %all_to_all.20 = bf16[64,2,256]{2,1,0:T(2,128)(2,1)S(1)} all-to-all(bf16[64,2,256]{2,1,0:T(2,128)(2,1)S(1)} %reshape.39), channel_id=1, replica_groups=mesh['z'=16,'x'=4,'y'=4,'core'=2] {'y','z'}, dimensions={0} | all-to-all | bytes 131072 | tf_op jit(solution)/shard_map/all_to_all | solution.py:228
  37.0 12.7 %all_to_all.21 = bf16[16,32,256]{2,1,0:T(8,128)(2,1)S(1)} all-to-all(bf16[16,32,256]{2,1,0:T(8,128)(2,1)S(1)} %broadcast_in_dim.4), channel_id=1, replica_groups=mesh['z'=16,'x'=4,'y'=4,'core'=2] {'x','y'}, dimensions={0} | all-to-all | bytes 524288 | tf_op jit(solution)/shard_map/all_to_all | solution.py:232
  49.7 0.0 copy-start.2
  49.7 5.0 %all-gather.1 = bf16[32,32,256]{2,1,0:T(8,128)(2,1)S(1)} all-gather(bf16[16,32,256]{2,1,0:T(8,128)(2,1)S(1)} %all_to_all.21), channel_id=3, replica_groups=mesh['z'=16,'x'=4,'y'=4,'core'=2] {'core'}, dimensions={0}, use_global_device_ids=true | all-gather | bytes 786432 | tf_op jit(solution)/shard_map/all_gather | solution.py:233
  54.7 0.0 copy-done
  54.7 0.0 copy-done.1
  54.7 0.0 copy-done.2
  54.7 0.8 expert.1
  55.6 2.2 %all-gather.2 = bf16[32,32,256]{2,1,0:T(8,128)(2,1)S(1)} all-gather(bf16[16,32,256]{2,1,0:T(8,128)(2,1)S(1)} %get-tuple-element.16), channel_id=4, replica_groups=mesh['z'=16,'x'=4,'y'=4,'core'=2] {'core'}, dimensions={0}, use_global_device_ids=true | all-gather | bytes 786432 | tf_op jit(solution)/shard_map/all_gather | solution.py:235
  57.8 0.1 fusion.1
  57.9 10.7 %all_to_all.22 = bf16[16,32,256]{2,1,0:T(8,128)(2,1)S(1)} all-to-all(bf16[16,32,256]{2,1,0:T(8,128)(2,1)S(1)} %fusion.1), channel_id=1, replica_groups=mesh['z'=16,'x'=4,'y'=4,'core'=2] {'x','y'}, dimensions={0} | all-to-all | bytes 524288 | tf_op jit(solution)/shard_map/all_to_all | solution.py:238
  68.7 13.8 %all_to_all.23 = bf16[16,2,256]{2,1,0:T(2,128)(2,1)S(1)} all-to-all(bf16[16,2,256]{2,1,0:T(2,128)(2,1)S(1)} %convert_element_type.70), channel_id=1, replica_groups=mesh['z'=16,'x'=4,'y'=4,'core'=2] {'z'}, dimensions={0} | all-to-all | bytes 32768 | tf_op jit(solution)/shard_map/all_to_all | solution.py:240
  82.5 0.7 multiply_reduce_fusion
  (10 shorter events, 0.2 us)
Async XLA Ops:
  10.4 44.3 %copy-start = (bf16[1,2048,256]{2,1,0:T(8,128)(2,1)S(1)}, bf16[1,2048,256]{2,1,0:T(8,128)(2,1)}, u32[]{:S(2)}) copy-start(bf16[1,2048,256]{2,1,0:T(8,128)(2,1)} %param.22) | copy-start | bytes 3145732
  10.4 44.3 %copy-start.1 = (bf16[1,256,2048]{2,1,0:T(8,128)(2,1)S(1)}, bf16[1,256,2048]{2,1,0:T(8,128)(2,1)}, u32[]{:S(2)}) copy-start(bf16[1,256,2048]{2,1,0:T(8,128)(2,1)} %param.23) | copy-start | bytes 3145732
  49.7 5.0 %copy-start.2 = (f32[2048]{0:T(1024)S(1)}, f32[2048]{0:T(1024)}, u32[]{:S(2)}) copy-start(f32[2048]{0:T(1024)} %param.19) | copy-start | bytes 24580
